TPU v7x, 32 devices: a whole 2x2x4 slice. The times are simulated.
32 devices in a mesh: dp: 8 (over z, y), chan: 4 (over x, core).
Axes of the slice: x: 2, y: 2, z: 4, core: 2. Of those that a mesh axis runs over, the one named last changes fastest.
Arguments:
- inputs: bfloat16 [262144, 256], P(('dp', 'chan')), may hold values from -6 to 6
- valid_mask: int32 [262144], P('dp'), may hold values from 0 to 1, as said below
- code_ids: int32 [262144], P(('dp', 'chan')), may hold values from 0 to 511
- cotangent: bfloat16 [262144, 256], P(('dp', 'chan')), may hold values from -6 to 6
- conv_weight: float32 [9, 256, 256], P(None, 'dp', 'chan'), may hold values from -0.125 to 0.125
- conv_first: float32 [9, 256, 256], P(None, 'dp', 'chan'), may hold values from -1024 to 1024
- conv_second: float32 [9, 256, 256], P(None, 'dp', 'chan'), may hold values from 26869.76 to 107479.04
- point_weight: float32 [256, 256], P('chan', 'dp'), may hold values from -0.375 to 0.375
- point_first: float32 [256, 256], P('chan', 'dp'), may hold values from -1024 to 1024
- point_second: float32 [256, 256], P('chan', 'dp'), may hold values from 26869.76 to 107479.04
- proj_weight: float32 [256, 64], P(('dp', 'chan')), may hold values from -0.375 to 0.375
- proj_first: float32 [256, 64], P(('dp', 'chan')), may hold values from -4096 to 4096
- proj_second: float32 [256, 64], P(('dp', 'chan')), may hold values from 568852.5 to 2275410
- code_book: float32 [512, 64], P(('dp', 'chan')), may hold values from -6 to 6
- code_first: float32 [512, 64], P(('dp', 'chan')), may hold values from -2560 to 2560
- code_second: float32 [512, 64], P(('dp', 'chan')), may hold values from 175636.48 to 705167.4
- dec_weight: float32 [256, 64], P(('dp', 'chan')), may hold values from -0.75 to 0.75
- dec_first: float32 [256, 64], P(('dp', 'chan')), may hold values from -2048 to 2048
- dec_second: float32 [256, 64], P(('dp', 'chan')), may hold values from 107479.04 to 429916.16
Outputs:
- output: bfloat16 [262144, 256], P(('dp', 'chan'))
- input_grad: bfloat16 [262144, 256], P(('dp', 'chan'))
- losses: float32 [2], replicated
- conv_new: float32 [9, 256, 256], P(None, 'dp', 'chan')
- conv_first_new: float32 [9, 256, 256], P(None, 'dp', 'chan')
- conv_second_new: float32 [9, 256, 256], P(None, 'dp', 'chan')
- conv_copy: bfloat16 [9, 256, 256], P(None, 'dp', 'chan')
- point_new: float32 [256, 256], P('chan', 'dp')
- point_first_new: float32 [256, 256], P('chan', 'dp')
- point_second_new: float32 [256, 256], P('chan', 'dp')
- point_copy: bfloat16 [256, 256], P('chan', 'dp')
- proj_new: float32 [256, 64], P(('dp', 'chan'))
- proj_first_new: float32 [256, 64], P(('dp', 'chan'))
- proj_second_new: float32 [256, 64], P(('dp', 'chan'))
- proj_copy: bfloat16 [256, 64], P(('dp', 'chan'))
- code_new: float32 [512, 64], P(('dp', 'chan'))
- code_first_new: float32 [512, 64], P(('dp', 'chan'))
- code_second_new: float32 [512, 64], P(('dp', 'chan'))
- code_copy: bfloat16 [512, 64], P(('dp', 'chan'))
- dec_new: float32 [256, 64], P(('dp', 'chan'))
- dec_first_new: float32 [256, 64], P(('dp', 'chan'))
- dec_second_new: float32 [256, 64], P(('dp', 'chan'))
- dec_copy: bfloat16 [256, 64], P(('dp', 'chan'))
Inputs may be any that keep to these rules, and one draw needn't show every extreme that they name: The canvas of each index of dp holds 2 tiles of 128 x 128 pixels side by side (tile b covers columns b * 128 to (b + 1) * 128 - 1). In each index of dp one tile, drawn from the seed, holds one image in its top left corner that is 112 rows tall and between 16 and 112 columns wide. Every other tile holds one square image of side s in its top left corner or, where s < 64, four of side s at row and column offsets 0 and 64, with s between 16 and 112. valid_mask is 1 on the images' pixels.
All inputs are finite; a program needn't handle non-finite values.
Results may differ from a plain program's by a relative error of at most 0.0044.
The roundings to bfloat16 on the way count: a program that leaves them out, or rounds other values in their place, can miss the bound.
Values may be sent and summed in bfloat16 or wider, within the bound.
A program may use at most 256 MiB of HBM per device.

v0:
```python
import jax
import jax.numpy as jnp
from jax import lax
from jax.sharding import PartitionSpec as P

LAT = 64
BAND = 128
BANDS = 2
STEP = 5


beta_first = 0.5
beta_second = 0.5
epsilon = 1e-08
decay_rate = 0.01


def row_stride():
    return BANDS * BAND


def tap_offsets():
    stride = row_stride()
    return [row_step * stride + col_step for row_step in (-1, 0, 1) for col_step in (-1, 0, 1)]


def conv_forward(padded, weights, row_count):
    margin = row_stride() + 1
    summed_terms = None
    for tap_index, offset in enumerate(tap_offsets()):
        begin = margin + offset
        window = lax.slice_in_dim(padded, begin, begin + row_count, axis=0)
        product = jnp.dot(window, weights[tap_index], preferred_element_type=jnp.float32)
        summed_terms = product if summed_terms is None else summed_terms + product
    return summed_terms


def conv_weight_grad(padded, grads, row_count):
    margin = row_stride() + 1
    products = []
    for offset in tap_offsets():
        begin = margin + offset
        window = lax.slice_in_dim(padded, begin, begin + row_count, axis=0)
        products.append(
            lax.dot_general(
                window, grads, (((0,), (0,)), ((), ())), preferred_element_type=jnp.float32
            )
        )
    return jnp.stack(products)


def conv_input_grad(padded_grads, weights, row_count):
    margin = row_stride() + 1
    summed_terms = None
    for tap_index, offset in enumerate(tap_offsets()):
        begin = margin - offset
        window = lax.slice_in_dim(padded_grads, begin, begin + row_count, axis=0)
        product = lax.dot_general(
            window, weights[tap_index], (((1,), (1,)), ((), ())), preferred_element_type=jnp.float32
        )
        summed_terms = product if summed_terms is None else summed_terms + product
    return summed_terms


def bottleneck(latent, mask_rows, code_rows, cotangent, codebook, decoder):
    weight_rows = mask_rows.astype(jnp.float32)[:, None]
    entries = jnp.arange(codebook.shape[0], dtype=jnp.int32)
    onehot = (code_rows[:, None] == entries[None, :]).astype(jnp.bfloat16)
    chosen = jnp.dot(onehot, codebook, preferred_element_type=jnp.float32)
    gap_rows = latent - chosen
    loss_part = jnp.sum(weight_rows * gap_rows * gap_rows)
    count_part = jnp.sum(weight_rows)
    decoded = chosen.astype(jnp.bfloat16)
    decoded_out = lax.dot_general(
        decoded, decoder, (((1,), (1,)), ((), ())), preferred_element_type=jnp.float32
    )
    output = (decoded_out * weight_rows).astype(jnp.bfloat16)
    kept_rows = cotangent * mask_rows.astype(jnp.bfloat16)[:, None]
    decoded_grad = jnp.dot(kept_rows, decoder, preferred_element_type=jnp.float32)
    latent_grad = (decoded_grad + 0.5 * weight_rows * gap_rows).astype(jnp.bfloat16)
    decoder_grad = lax.dot_general(
        kept_rows, decoded, (((0,), (0,)), ((), ())), preferred_element_type=jnp.float32
    )
    book_term = -2.0 * weight_rows * gap_rows
    high_part = book_term.astype(jnp.bfloat16)
    rest_term = book_term - high_part.astype(jnp.float32)
    middle_part = rest_term.astype(jnp.bfloat16)
    low_part = (rest_term - middle_part.astype(jnp.float32)).astype(jnp.bfloat16)
    stacked = jnp.concatenate([high_part, middle_part, low_part], axis=1)
    book_parts = lax.dot_general(
        onehot, stacked, (((0,), (0,)), ((), ())), preferred_element_type=jnp.float32
    )
    width = book_term.shape[1]
    book_grad = book_parts[:, :width] + (
        book_parts[:, width : 2 * width] + book_parts[:, 2 * width :]
    )
    return (output, latent_grad, decoder_grad, book_grad, loss_part, count_part)


def adamw(grad, weight, first, second, rate):
    first_new = beta_first * first + (1.0 - beta_first) * grad
    second_new = beta_second * second + (1.0 - beta_second) * grad * grad
    first_hat = first_new / (1.0 - beta_first**STEP)
    second_hat = second_new / (1.0 - beta_second**STEP)
    weight_new = weight - rate * (
        first_hat / (jnp.sqrt(second_hat) + epsilon) + decay_rate * weight
    )
    return (weight_new, first_new, second_new, weight_new.astype(jnp.bfloat16))


def on_device(
    inputs,
    valid_mask,
    code_ids,
    cotangent,
    conv_weight,
    conv_first,
    conv_second,
    point_weight,
    point_first,
    point_second,
    proj_weight,
    proj_first,
    proj_second,
    code_book,
    code_first,
    code_second,
    dec_weight,
    dec_first,
    dec_second,
):
    chan_count = lax.axis_size("chan")
    chan_index = lax.axis_index("chan")
    rows_quarter = inputs.shape[0]
    rows_all = valid_mask.shape[0]
    channels = inputs.shape[1]
    chan_width = channels // chan_count
    margin = row_stride() + 1
    conv_low, point_low = (
        lax.all_gather(conv_weight.astype(jnp.bfloat16), "dp", axis=1, tiled=True),
        lax.all_gather(point_weight.astype(jnp.bfloat16), "dp", axis=1, tiled=True),
    )
    proj_full, book_full, dec_full = (
        lax.all_gather(proj_weight.astype(jnp.bfloat16), ("dp", "chan"), axis=0, tiled=True),
        lax.all_gather(code_book.astype(jnp.bfloat16), ("dp", "chan"), axis=0, tiled=True),
        lax.all_gather(dec_weight.astype(jnp.bfloat16), ("dp", "chan"), axis=0, tiled=True),
    )
    mask_rows = lax.dynamic_slice_in_dim(valid_mask, chan_index * rows_quarter, rows_quarter)
    first_column = chan_index * chan_width
    gathered = lax.all_gather(inputs, "chan", axis=0, tiled=True)
    valid_all = (valid_mask > 0)[:, None]
    activations = jnp.where(valid_all, jnp.maximum(gathered, 0), 0)
    padded = jnp.pad(activations, ((margin, margin), (0, 0)))
    hidden = conv_forward(padded, conv_low, rows_all)
    middle = jnp.maximum(hidden, 0.0).astype(jnp.bfloat16)
    partial_branch = jnp.dot(middle, point_low, preferred_element_type=jnp.float32)
    branch = lax.psum_scatter(partial_branch, "chan", scatter_dimension=1, tiled=True)
    own_inputs = lax.dynamic_slice_in_dim(gathered, first_column, chan_width, 1).astype(jnp.float32)
    summed = (own_inputs + branch).astype(jnp.bfloat16)
    proj_rows = lax.dynamic_slice_in_dim(proj_full, first_column, chan_width, 0)
    window = summed
    latent = lax.psum_scatter(
        jnp.dot(window, proj_rows, preferred_element_type=jnp.float32),
        "chan",
        scatter_dimension=0,
        tiled=True,
    )
    output, latent_grad, decoder_grad, book_grad, loss_part, count_part = bottleneck(
        latent, mask_rows, code_ids, cotangent, book_full, dec_full
    )
    grads_all = lax.all_gather(latent_grad, "chan", axis=0, tiled=True)
    proj_part = lax.dot_general(
        summed, grads_all, (((0,), (0,)), ((), ())), preferred_element_type=jnp.float32
    )
    proj_grad = lax.dynamic_update_slice_in_dim(
        jnp.zeros((channels, proj_part.shape[1]), jnp.float32), proj_part, first_column, 0
    )
    resid = lax.dot_general(
        grads_all, proj_rows, (((1,), (1,)), ((), ())), preferred_element_type=jnp.float32
    )
    resid_all = lax.all_gather(resid.astype(jnp.bfloat16), "chan", axis=1, tiled=True)
    point_grad = lax.dot_general(
        middle, resid_all, (((0,), (0,)), ((), ())), preferred_element_type=jnp.float32
    )
    hidden_back = lax.dot_general(
        resid_all, point_low, (((1,), (1,)), ((), ())), preferred_element_type=jnp.float32
    )
    hidden_grad = jnp.where(hidden > 0.0, hidden_back.astype(jnp.bfloat16), 0)
    conv_grad = conv_weight_grad(padded, hidden_grad, rows_all)
    grad_padded = jnp.pad(hidden_grad, ((margin, margin), (0, 0)))
    slopes = jnp.logical_and(gathered > 0, valid_all)
    window = grad_padded
    back_grad = conv_input_grad(window, conv_low, rows_quarter * lax.axis_size("chan"))
    back_grad = jnp.where(slopes, back_grad, 0.0)
    own_back = lax.dynamic_slice_in_dim(back_grad, first_column, chan_width, 1)
    input_grad = lax.psum_scatter(
        lax.dynamic_update_slice_in_dim(back_grad, own_back + resid, first_column, 1),
        "chan",
        scatter_dimension=0,
        tiled=True,
    ).astype(jnp.bfloat16)
    conv_reduced, point_reduced = (
        lax.psum_scatter(conv_grad, "dp", scatter_dimension=1, tiled=True),
        lax.psum_scatter(point_grad, "dp", scatter_dimension=1, tiled=True),
    )
    proj_reduced, book_reduced, dec_reduced = (
        lax.psum_scatter(proj_grad, ("dp", "chan"), scatter_dimension=0, tiled=True),
        lax.psum_scatter(book_grad, ("dp", "chan"), scatter_dimension=0, tiled=True),
        lax.psum_scatter(decoder_grad, ("dp", "chan"), scatter_dimension=0, tiled=True),
    )
    loss_total, count_total = lax.psum((loss_part, count_part), ("dp", "chan"))
    losses = jnp.stack([loss_total, 0.25 * loss_total]) / (count_total * LAT)
    conv_out = adamw(conv_reduced, conv_weight, conv_first, conv_second, 0.01)
    point_out = adamw(point_reduced, point_weight, point_first, point_second, 0.03)
    proj_out = adamw(proj_reduced, proj_weight, proj_first, proj_second, 0.03)
    code_out = adamw(book_reduced, code_book, code_first, code_second, 0.5)
    dec_out = adamw(dec_reduced, dec_weight, dec_first, dec_second, 0.06)
    return (
        output,
        input_grad,
        losses,
        conv_out[0],
        conv_out[1],
        conv_out[2],
        conv_out[3],
        point_out[0],
        point_out[1],
        point_out[2],
        point_out[3],
        proj_out[0],
        proj_out[1],
        proj_out[2],
        proj_out[3],
        code_out[0],
        code_out[1],
        code_out[2],
        code_out[3],
        dec_out[0],
        dec_out[1],
        dec_out[2],
        dec_out[3],
    )


def solution(mesh):
    in_specs = (
        P(("dp", "chan"), None),
        P("dp"),
        P(("dp", "chan")),
        P(("dp", "chan"), None),
        P(None, "dp", "chan"),
        P(None, "dp", "chan"),
        P(None, "dp", "chan"),
        P("chan", "dp"),
        P("chan", "dp"),
        P("chan", "dp"),
        P(("dp", "chan"), None),
        P(("dp", "chan"), None),
        P(("dp", "chan"), None),
        P(("dp", "chan"), None),
        P(("dp", "chan"), None),
        P(("dp", "chan"), None),
        P(("dp", "chan"), None),
        P(("dp", "chan"), None),
        P(("dp", "chan"), None),
    )
    out_specs = (
        P(("dp", "chan"), None),
        P(("dp", "chan"), None),
        P(),
        P(None, "dp", "chan"),
        P(None, "dp", "chan"),
        P(None, "dp", "chan"),
        P(None, "dp", "chan"),
        P("chan", "dp"),
        P("chan", "dp"),
        P("chan", "dp"),
        P("chan", "dp"),
        P(("dp", "chan"), None),
        P(("dp", "chan"), None),
        P(("dp", "chan"), None),
        P(("dp", "chan"), None),
        P(("dp", "chan"), None),
        P(("dp", "chan"), None),
        P(("dp", "chan"), None),
        P(("dp", "chan"), None),
        P(("dp", "chan"), None),
        P(("dp", "chan"), None),
        P(("dp", "chan"), None),
        P(("dp", "chan"), None),
    )
    return jax.shard_map(
        on_device, mesh=mesh, in_specs=in_specs, out_specs=out_specs, check_vma=False
    )
```

profile of v0, /device:TPU:0, one launch (start us, length us, event | category | flops | bytes accessed | tf_op | source)
XLA Modules:
  0.0 1406.2 jit_solution(18092275970742368631)
XLA Ops:
  13.8 32.3 %all_gather.28 = bf16[64,256]{0,1:T(8,128)(2,1)S(1)} all-gather(bf16[64,32]{0,1:T(8,128)(2,1)S(1)} %convert_element_type.96), channel_id=1, replica_groups=mesh['dp'=8,'chan'=4] {'dp'}, dimensions={1}, use_global_device_ids=true | all-gather | bytes 36864 | tf_op jit(solution)/shard_map/all_gather | solution.py:141
  46.1 31.4 %all_gather.27 = bf16[9,256,64]{2,1,0:T(8,128)(2,1)S(1)} all-gather(bf16[9,32,64]{2,1,0:T(8,128)(2,1)S(1)} %convert_element_type.92), channel_id=1, replica_groups=mesh['dp'=8,'chan'=4] {'dp'}, dimensions={1}, use_global_device_ids=true | all-gather | bytes 331776 | tf_op jit(solution)/shard_map/all_gather | solution.py:140
  77.5 45.0 %all-gather.4.cloned.1.call-done = bf16[32768,256]{0,1:T(8,128)(2,1)} async-done(((bf16[8192,256]{0,1:T(8,128)(2,1)}), bf16[32768,256]{0,1:T(8,128)(2,1)}) %all-gather.4.cloned.1.call-update) | async-done | bytes 16777232 | tf_op jit(solution)/shard_map/all_gather | solution.py:150
  154.7 11.4 convolution_add_fusion.14
  166.1 11.3 convolution_add_fusion.13
  177.4 12.2 convolution_add_fusion.12
  212.0 13.3 convolution_add_fusion.9
  225.3 11.3 convolution_add_fusion.8
  239.9 13.1 fusion.54
  253.6 40.7 %all_gather.29 = bf16[256,64]{1,0:T(8,128)(2,1)S(1)} all-gather(bf16[8,64]{1,0:T(8,128)(2,1)S(1)} %convert_element_type.98), channel_id=1, replica_groups=mesh['dp'=8,'chan'=4] {'dp','chan'}, dimensions={0}, use_global_device_ids=true | all-gather | bytes 33792 | tf_op jit(solution)/shard_map/all_gather | solution.py:144
  294.3 193.7 %reduce-scatter.9.cloned.1.call-done = f32[32768,64]{0,1:T(8,128)} async-done(((f32[32768,256]{0,1:T(8,128)}), f32[32768,64]{0,1:T(8,128)}) %reduce-scatter.9.cloned.1.call-update) | async-done | bytes 8388624 | tf_op jit(solution)/shard_map/reduce_scatter | solution.py:157
  497.9 41.1 %all_gather.25 = bf16[256,64]{1,0:T(8,128)(2,1)S(1)} all-gather(bf16[8,64]{1,0:T(8,128)(2,1)S(1)} %convert_element_type.89), channel_id=1, replica_groups=mesh['dp'=8,'chan'=4] {'dp','chan'}, dimensions={0}, use_global_device_ids=true | all-gather | bytes 33792 | tf_op jit(solution)/shard_map/all_gather | solution.py:146
  538.9 37.5 %all_gather.24 = bf16[512,64]{1,0:T(8,128)(2,1)S(1)} all-gather(bf16[16,64]{1,0:T(8,128)(2,1)S(1)} %convert_element_type.87), channel_id=1, replica_groups=mesh['dp'=8,'chan'=4] {'dp','chan'}, dimensions={0}, use_global_device_ids=true | all-gather | bytes 67584 | tf_op jit(solution)/shard_map/all_gather | solution.py:145
  586.0 32.2 %all-gather.6.cloned.1.call-done = bf16[32768,64]{0,1:T(8,128)(2,1)} async-done(((bf16[8192,64]{0,1:T(8,128)(2,1)}), bf16[32768,64]{0,1:T(8,128)(2,1)}) %all-gather.6.cloned.1.call-update) | async-done | bytes 4194320 | tf_op jit(solution)/shard_map/all_gather | solution.py:171
  650.5 82.0 %all-gather.8.cloned.1.call-done = bf16[32768,256]{0,1:T(8,128)(2,1)} async-done(((bf16[32768,64]{0,1:T(8,128)(2,1)}), bf16[32768,256]{0,1:T(8,128)(2,1)}) %all-gather.8.cloned.1.call-update) | async-done | bytes 16777232 | tf_op jit(solution)/shard_map/all_gather | solution.py:181
  732.5 11.3 fusion.1
  745.8 11.8 fusion.59
  757.6 15.6 %fusion.40 = f32[32768,256]{0,1:T(8,128)} fusion(bf16[32768,64]{0,1:T(8,128)(2,1)} %copy-done.1, bf16[9,256,64]{2,1,0:T(8,128)(2,1)S(1)} %all_gather.27), kind=kOutput, calls=%fused_computation.64 | convolution fusion | flops 1073741824 | bytes 37814272 | tf_op jit(solution)/shard_map/dot_general | solution.py:58
  773.1 11.5 fusion.65
  821.0 26.1 %convolution_add_fusion.7 = f32[32768,256]{0,1:T(8,128)} fusion(f32[32768,256]{0,1:T(8,128)} %fusion.40, bf16[32768,64]{0,1:T(8,128)(2,1)} %copy-done.1, bf16[9,256,64]{2,1,0:T(8,128)(2,1)S(1)} %all_gather.27), kind=kOutput, calls=%fused_computation.7 | convolution fusion | flops 1082130432 | bytes 71368704 | tf_op jit(solution)/shard_map/dot_general | solution.py:58
  847.1 24.6 %convolution_add_fusion.6 = f32[32768,256]{0,1:T(8,128)} fusion(f32[32768,256]{0,1:T(8,128)} %convolution_add_fusion.7, bf16[32768,64]{0,1:T(8,128)(2,1)S(1)} %copy-done.3, bf16[9,256,64]{2,1,0:T(8,128)(2,1)S(1)} %all_gather.27), kind=kOutput, calls=%fused_computation.6 | convolution fusion | flops 1082130432 | bytes 71368704 | tf_op jit(solution)/shard_map/dot_general | solution.py:58
  871.7 24.7 %convolution_add_fusion.5 = f32[32768,256]{0,1:T(8,128)} fusion(f32[32768,256]{0,1:T(8,128)} %convolution_add_fusion.6, bf16[32768,64]{0,1:T(8,128)(2,1)S(1)} %copy-done.3, bf16[9,256,64]{2,1,0:T(8,128)(2,1)S(1)} %all_gather.27), kind=kOutput, calls=%fused_computation.5 | convolution fusion | flops 1082130432 | bytes 71368704 | tf_op jit(solution)/shard_map/dot_general | solution.py:58
  896.4 24.7 %convolution_add_fusion.4 = f32[32768,256]{0,1:T(8,128)} fusion(f32[32768,256]{0,1:T(8,128)} %convolution_add_fusion.5, bf16[32768,64]{0,1:T(8,128)(2,1)S(1)} %copy-done.3, bf16[9,256,64]{2,1,0:T(8,128)(2,1)S(1)} %all_gather.27), kind=kOutput, calls=%fused_computation.4 | convolution fusion | flops 1082130432 | bytes 71368704 | tf_op jit(solution)/shard_map/dot_general | solution.py:58
  921.2 24.7 %convolution_add_fusion.3 = f32[32768,256]{0,1:T(8,128)} fusion(f32[32768,256]{0,1:T(8,128)} %convolution_add_fusion.4, bf16[32768,64]{0,1:T(8,128)(2,1)S(1)} %copy-done.3, bf16[9,256,64]{2,1,0:T(8,128)(2,1)S(1)} %all_gather.27), kind=kOutput, calls=%fused_computation.3 | convolution fusion | flops 1082130432 | bytes 71368704 | tf_op jit(solution)/shard_map/dot_general | solution.py:58
  945.8 24.6 %convolution_add_fusion.2 = f32[32768,256]{0,1:T(8,128)} fusion(f32[32768,256]{0,1:T(8,128)} %convolution_add_fusion.3, bf16[32768,64]{0,1:T(8,128)(2,1)S(1)} %copy-done.3, bf16[9,256,64]{2,1,0:T(8,128)(2,1)S(1)} %all_gather.27), kind=kOutput, calls=%fused_computation.2 | convolution fusion | flops 1082130432 | bytes 71368704 | tf_op jit(solution)/shard_map/dot_general | solution.py:58
  970.5 24.6 %convolution_add_fusion.1 = f32[32768,256]{0,1:T(8,128)} fusion(f32[32768,256]{0,1:T(8,128)} %convolution_add_fusion.2, bf16[32768,64]{0,1:T(8,128)(2,1)S(1)} %copy-done.3, bf16[9,256,64]{2,1,0:T(8,128)(2,1)S(1)} %all_gather.27), kind=kOutput, calls=%fused_computation.1 | convolution fusion | flops 1082130432 | bytes 71368704 | tf_op jit(solution)/shard_map/dot_general | solution.py:58
  995.1 13.3 fusion.53
  1019.0 13.1 fusion.101
  1034.7 30.1 %fusion = f32[32768,256]{0,1:T(8,128)} fusion(f32[32768,256]{0,1:T(8,128)} %convolution_add_fusion.1, bf16[32768,256]{0,1:T(8,128)(2,1)} %all-gather.4.cloned.1.call-done, pred[32768]{0:T(1024)(128)(4,1)S(1)} %copy-done.18, bf16[32768,64]{0,1:T(8,128)(2,1)} %copy-done.1, bf16[9,256,64]{2,1,0:T(8,128)(2,1)S(1)} %all_gather.27), kind=kOutput, calls=%fused_computation.8 | convolution fusion | flops 1124073472 | bytes 88178688 | tf_op jit(solution)/shard_map/dot_general | solution.py:58
  1074.9 40.3 %all-reduce.4 = (f32[]{:T(128)}, f32[]{:T(128)}) all-reduce(f32[]{:T(128)} %get-tuple-element.122, f32[]{:T(128)} %get-tuple-element.123), channel_id=1, replica_groups=mesh['dp'=8,'chan'=4] {'dp','chan'}, use_global_device_ids=true, to_apply=%region_4.5 | all-reduce | flops 2 | bytes 16 | tf_op jit(solution)/shard_map/psum | solution.py:211
  1125.0 25.5 %reduce-scatter.15.cloned.1.call-done = f32[9,32,64]{2,0,1:T(8,128)} async-done(((f32[9,256,64]{2,0,1:T(8,128)}), f32[9,32,64]{2,0,1:T(8,128)}) %reduce-scatter.15.cloned.1.call-update) | async-done | bytes 73744 | tf_op jit(solution)/shard_map/reduce_scatter | solution.py:203
  1152.3 234.5 %reduce-scatter.13.cloned.1.call-done = f32[8192,256]{0,1:T(8,128)} async-done(((f32[32768,256]{0,1:T(8,128)}), f32[8192,256]{0,1:T(8,128)}) %reduce-scatter.13.cloned.1.call-update) | async-done | bytes 8388624 | tf_op jit(solution)/shard_map/reduce_scatter | solution.py:196
  (153 shorter events, 200.7 us)
Async XLA Ops:
  7.2 70.2 %copy-start.19 = (s32[32768]{0:T(1024)S(1)}, s32[32768]{0:T(1024)}, u32[]{:S(2)}) copy-start(s32[32768]{0:T(1024)} %param.20) | copy-start | bytes 393220
  7.2 115.2 %all-gather.4.cloned.1.call-start = ((), (), s32[]{:S(2)}) async-start(), calls=%async_computation.6 | async-start | bytes 20971520 | tf_op jit(solution)/shard_map/all_gather | solution.py:150
  13.7 474.3 %reduce-scatter.9.cloned.1.call-start = ((), (), s32[]{:S(2)}) async-start(), calls=%async_computation.7 | async-start | bytes 41943040 | tf_op jit(solution)/shard_map/reduce_scatter | solution.py:157
  77.5 53.2 %copy-start.17 = (pred[32768]{0:T(1024)(128)(4,1)}, pred[32768]{0:T(1024)(128)(4,1)S(1)}, u32[]{:S(2)}) copy-start(pred[32768]{0:T(1024)(128)(4,1)S(1)} %broadcast_compare_fusion) | copy-start | bytes 98308
  252.9 324.1 %reduce-scatter.11.cloned.1.call-start = ((), (), s32[]{:S(2)}) async-start(), calls=%async_computation.8 | async-start | bytes 10485760 | tf_op jit(solution)/shard_map/reduce_scatter | solution.py:162
  497.1 79.9 %copy-start.38 = (s32[8192]{0:T(1024)S(1)}, s32[8192]{0:T(1024)}, u32[]{:S(2)}) copy-start(s32[8192]{0:T(1024)} %param.21) | copy-start | bytes 98308
  497.2 121.0 %all-gather.6.cloned.1.call-start = ((), (), s32[]{:S(2)}) async-start(), calls=%async_computation.9 | async-start | bytes 5242880 | tf_op jit(solution)/shard_map/all_gather | solution.py:171
  538.9 47.0 %copy-start.10 = (bf16[256,64]{1,0:T(8,128)(2,1)}, bf16[256,64]{1,0:T(8,128)(2,1)S(1)}, u32[]{:S(2)}) copy-start(bf16[256,64]{1,0:T(8,128)(2,1)S(1)} %all_gather.25) | copy-start | bytes 98308
  576.4 50.0 %copy-start.8 = (f32[8192]{0:T(1024)}, f32[8192]{0:T(1024)S(1)}, u32[]{:S(2)}) copy-start(f32[8192]{0:T(1024)S(1)} %get-tuple-element.107) | copy-start | bytes 98308
  586.0 146.5 %all-gather.8.cloned.1.call-start = ((), (), s32[]{:S(2)}) async-start(), calls=%async_computation.10 | async-start | bytes 20971520 | tf_op jit(solution)/shard_map/all_gather | solution.py:181
  626.4 494.5 %reduce-scatter.19.cloned.1.call-start = ((), (), s32[]{:S(2)}) async-start(), calls=%async_computation.14 | async-start | bytes 270336 | tf_op jit(solution)/shard_map/reduce_scatter | solution.py:208
  641.7 480.5 %all-reduce.8.cloned.1.call-start = ((), (), s32[]{:S(2)}) async-start(), calls=%async_computation.15 | async-start | bytes 524288
  650.5 473.1 %reduce-scatter.17.cloned.1.call-start = ((), (), s32[]{:S(2)}) async-start(), calls=%async_computation.13 | async-start | bytes 147456 | tf_op jit(solution)/shard_map/reduce_scatter | solution.py:204
  1019.0 131.5 %reduce-scatter.15.cloned.1.call-start = ((), (), s32[]{:S(2)}) async-start(), calls=%async_computation.12 | async-start | bytes 2359296 | tf_op jit(solution)/shard_map/reduce_scatter | solution.py:203
  1034.6 352.2 %reduce-scatter.13.cloned.1.call-start = ((), (), s32[]{:S(2)}) async-start(), calls=%async_computation.11 | async-start | bytes 41943040 | tf_op jit(solution)/shard_map/reduce_scatter | solution.py:196
  1074.7 43.0 %copy-start.9 = (f32[8192]{0:T(1024)S(1)}, f32[8192]{0:T(1024)}, u32[]{:S(2)}) copy-start(f32[8192]{0:T(1024)} %copy-done.8) | copy-start | bytes 98308
  1074.7 43.0 %copy-start.11 = (bf16[256,64]{1,0:T(8,128)(2,1)S(1)}, bf16[256,64]{1,0:T(8,128)(2,1)}, u32[]{:S(2)}) copy-start(bf16[256,64]{1,0:T(8,128)(2,1)} %copy-done.10) | copy-start | bytes 98308
  1074.7 46.2 %copy-start.25 = (f32[16,64]{1,0:T(8,128)S(1)}, f32[16,64]{1,0:T(8,128)}, u32[]{:S(2)}) copy-start(f32[16,64]{1,0:T(8,128)} %param.32) | copy-start | bytes 12292
  1074.7 46.2 %copy-start.32 = (f32[16,64]{1,0:T(8,128)S(1)}, f32[16,64]{1,0:T(8,128)}, u32[]{:S(2)}) copy-start(f32[16,64]{1,0:T(8,128)} %param.33) | copy-start | bytes 12292
  1074.7 46.2 %copy-start.33 = (f32[16,64]{1,0:T(8,128)S(1)}, f32[16,64]{1,0:T(8,128)}, u32[]{:S(2)}) copy-start(f32[16,64]{1,0:T(8,128)} %param.34) | copy-start | bytes 12292
  1074.7 47.5 %copy-start.29 = (f32[8,64]{1,0:T(8,128)S(1)}, f32[8,64]{1,0:T(8,128)}, u32[]{:S(2)}) copy-start(f32[8,64]{1,0:T(8,128)} %param.35) | copy-start | bytes 6148
  1074.7 47.5 %copy-start.31 = (f32[8,64]{1,0:T(8,128)S(1)}, f32[8,64]{1,0:T(8,128)}, u32[]{:S(2)}) copy-start(f32[8,64]{1,0:T(8,128)} %param.29) | copy-start | bytes 6148
  1074.8 47.5 %copy-start.34 = (f32[8,64]{1,0:T(8,128)S(1)}, f32[8,64]{1,0:T(8,128)}, u32[]{:S(2)}) copy-start(f32[8,64]{1,0:T(8,128)} %param.36) | copy-start | bytes 6148
  1074.8 47.5 %copy-start.35 = (f32[8,64]{1,0:T(8,128)S(1)}, f32[8,64]{1,0:T(8,128)}, u32[]{:S(2)}) copy-start(f32[8,64]{1,0:T(8,128)} %param.37) | copy-start | bytes 6148
  1074.8 47.5 %copy-start.36 = (f32[8,64]{1,0:T(8,128)S(1)}, f32[8,64]{1,0:T(8,128)}, u32[]{:S(2)}) copy-start(f32[8,64]{1,0:T(8,128)} %param.31) | copy-start | bytes 6148
  1074.8 47.5 %copy-start.37 = (f32[8,64]{1,0:T(8,128)S(1)}, f32[8,64]{1,0:T(8,128)}, u32[]{:S(2)}) copy-start(f32[8,64]{1,0:T(8,128)} %param.30) | copy-start | bytes 6148
  1074.8 48.8 %copy-start.23 = (f32[64,32]{0,1:T(8,128)S(1)}, f32[64,32]{0,1:T(8,128)}, u32[]{:S(2)}) copy-start(f32[64,32]{0,1:T(8,128)} %param.26) | copy-start | bytes 24580
  1074.8 48.8 %copy-start.26 = (f32[64,32]{0,1:T(8,128)S(1)}, f32[64,32]{0,1:T(8,128)}, u32[]{:S(2)}) copy-start(f32[64,32]{0,1:T(8,128)} %param.27) | copy-start | bytes 24580
  1074.8 48.8 %copy-start.27 = (f32[64,32]{0,1:T(8,128)S(1)}, f32[64,32]{0,1:T(8,128)}, u32[]{:S(2)}) copy-start(f32[64,32]{0,1:T(8,128)} %param.28) | copy-start | bytes 24580
  1074.8 75.6 %copy-start.13 = (f32[9,32,64]{2,1,0:T(8,128)S(1)}, f32[9,32,64]{2,1,0:T(8,128)}, u32[]{:S(2)}) copy-start(f32[9,32,64]{2,1,0:T(8,128)} %param.23) | copy-start | bytes 221188
  1074.9 75.6 %copy-start.20 = (f32[9,32,64]{2,1,0:T(8,128)S(1)}, f32[9,32,64]{2,1,0:T(8,128)}, u32[]{:S(2)}) copy-start(f32[9,32,64]{2,1,0:T(8,128)} %param.24) | copy-start | bytes 221188
  1074.9 75.6 %copy-start.21 = (f32[9,32,64]{2,1,0:T(8,128)S(1)}, f32[9,32,64]{2,1,0:T(8,128)}, u32[]{:S(2)}) copy-start(f32[9,32,64]{2,1,0:T(8,128)} %param.25) | copy-start | bytes 221188
  (21 other events, 270.1 us)
Sparse Core Ops, SparseCore 0:
  13.8 108.6 all-gather.3
  253.1 234.8 reduce-scatter.8
  497.3 73.0 reduce-scatter.10
  586.1 32.0 all-gather.5
  626.5 105.9 all-gather.7
  734.7 133.5 reduce-scatter.18
  874.5 121.1 all-reduce.7
  1019.1 60.7 reduce-scatter.16
  1083.5 66.9 reduce-scatter.14
  1152.9 233.8 reduce-scatter.12
where the time goes:
time: 1420 us; the launch traced here: 1410 us
  waiting for transfers between devices  613 us (43%)
  matrix products  491 us (35%)
  blocking collectives  223 us (16%)
  other arithmetic  33 us (2%)
  local copies, waits for them, and re-layouts  29.2 us (2%)
  between operations  16.3 us (1%)
    reduce_scatter x1, waiting for transfers between devices, on_device(): lax.psum_scatter(lax.dynamic_update_slice_in_dim(back_grad, own_back + re...  235 us
    dot_general x9, matrix products, conv_input_grad(): lax.dot_general(window, weights[tap_index], (((1,), (1,)), ((), ())), pre...  220 us
    reduce_scatter x1, waiting for transfers between devices, on_device(): lax.psum_scatter(partial_branch, 'chan', scatter_dimension=1, tiled=True)  194 us
    dot_general x9, matrix products, conv_forward(): jnp.dot(window, weights[tap_index], preferred_element_type=jnp.float32)  100 us
    dot_general x9, matrix products, conv_weight_grad(): lax.dot_general(window, grads, (((0,), (0,)), ((), ())), preferred_elemen...  83.1 us
    all_gather x1, waiting for transfers between devices, on_device(): lax.all_gather(resid.astype(jnp.bfloat16), 'chan', axis=1, tiled=True)  82 us
    all_gather x1, waiting for transfers between devices, on_device(): gathered = lax.all_gather(inputs, 'chan', axis=0, tiled=True)  45 us
    all_gather x1, blocking collectives, on_device(): lax.all_gather(dec_weight.astype(jnp.bfloat16), ('dp', 'chan'), axis=0, t...  41.1 us
  transfers between devices with their start and end apart: 10, of which 6 were waited for; matrix products, arithmetic and copies ran while one was open for 27% of the time, Pallas kernels for 0%

commit v1 on v0

--- a/solution.py
+++ b/solution.py
@@ -1,18 +1,784 @@
+import functools
+
 import jax
 import jax.numpy as jnp
 from jax import lax
+from jax.experimental import pallas as pl
+from jax.experimental.pallas import tpu as pltpu
 from jax.sharding import PartitionSpec as P
 
 LAT = 64
 BAND = 128
 BANDS = 2
 STEP = 5
-
+SIDE = BAND
+PITCH = BANDS * SIDE
+CHUNK_ROWS = 4
+CHUNK = CHUNK_ROWS * PITCH
+MESH = pl.DeviceIdType.MESH
+F32 = jnp.float32
+BF16 = jnp.bfloat16
 
 beta_first = 0.5
 beta_second = 0.5
 epsilon = 1e-08
 decay_rate = 0.01
+
+
+def adamw(grad, weight, first, second, rate):
+    first_new = beta_first * first + (1.0 - beta_first) * grad
+    second_new = beta_second * second + (1.0 - beta_second) * grad * grad
+    first_hat = first_new / (1.0 - beta_first**STEP)
+    second_hat = second_new / (1.0 - beta_second**STEP)
+    weight_new = weight - rate * (
+        first_hat / (jnp.sqrt(second_hat) + epsilon) + decay_rate * weight
+    )
+    return (weight_new, first_new, second_new, weight_new.astype(BF16))
+
+
+def dot(a, b):
+    return jnp.dot(a, b, preferred_element_type=F32)
+
+
+def dot_rows(a, b):
+    return lax.dot_general(a, b, (((0,), (0,)), ((), ())), preferred_element_type=F32)
+
+
+def aligned(value, unit):
+    return pl.multiple_of(value, unit)
+
+
+def block_kernel(
+    rows,
+    x_hbm,
+    cot_hbm,
+    ids_ref,
+    mask_ref,
+    conv_ref,
+    point_ref,
+    proj_ref,
+    book_ref,
+    dec_ref,
+    ub_hbm,
+    ig_hbm,
+    g_ref,
+    q_ref,
+    dz_ref,
+    xv,
+    xhalo,
+    cotv,
+    shifted,
+    mask_rows,
+    col_mask,
+    u_rows,
+    ub_rows,
+    lg_rows,
+    hgp,
+    hgt,
+    wsend,
+    wpre,
+    wb,
+    pb,
+    wfull,
+    wback,
+    point_t,
+    point_n,
+    qf,
+    bookf,
+    decz,
+    projz,
+    proj_t,
+    book_t,
+    dec_acc,
+    proj_acc,
+    point_acc,
+    book_acc,
+    loss_acc,
+    gp,
+    gs,
+    rp0,
+    rp1,
+    rp2,
+    rc0,
+    rc1,
+    rc2,
+    fin,
+    rx3,
+    x_sem,
+    cot_sem,
+    out_sem,
+    ub_sem,
+    halo_s,
+    halo_r,
+    ag_s,
+    ag_r,
+    rs_s,
+    rs_r,
+):
+    dp, chan = lax.axis_index("dp"), lax.axis_index("chan")
+    core, xc = lax.rem(chan, 2), lax.div(chan, 2)
+    yc, zc = lax.rem(dp, 2), lax.div(dp, 2)
+    core_peer = (dp, chan + 1 - 2 * core)
+
+    def xy_of(k):
+        x_new = 1 - xc if k % 2 else xc
+        y_new = 1 - yc if k // 2 else yc
+        return x_new, y_new
+
+    def xy_peer(k):
+        x_new, y_new = xy_of(k)
+        return (2 * zc + y_new, 2 * x_new + core)
+
+    def z_of(k):
+        if k == 1:
+            return zc + 1 - 2 * lax.rem(zc, 2)
+        if k == 2:
+            return lax.rem(zc + 2, 4)
+        return 3 - zc
+
+    def z_peer(k):
+        return (2 * z_of(k) + yc, chan)
+
+    up_peer, down_peer = (dp, chan - 1), (dp, chan + 1)
+    chunks = rows // CHUNK_ROWS
+    pixels = rows * PITCH
+    pending = []
+
+    def send(src, dst, s_sem, r_sem, peer):
+        copy = pltpu.make_async_remote_copy(
+            src_ref=src, dst_ref=dst, send_sem=s_sem, recv_sem=r_sem, device_id=peer, device_id_type=MESH
+        )
+        copy.start()
+        pending.append(copy)
+        return copy
+
+    def x_copy(k):
+        part = pl.ds(k * CHUNK_ROWS, CHUNK_ROWS)
+        return pltpu.make_async_copy(x_hbm.at[part, :, pl.ds(0, SIDE), :], xv.at[part], x_sem.at[k])
+
+    def cot_copy(k):
+        part = pl.ds(k * CHUNK_ROWS, CHUNK_ROWS)
+        return pltpu.make_async_copy(cot_hbm.at[part, :, pl.ds(0, SIDE), :], cotv.at[part], cot_sem.at[k])
+
+    for k in range(chunks):
+        x_copy(k).start()
+    for k in range(chunks):
+        cot_copy(k).start()
+
+    lane = lax.broadcasted_iota(jnp.int32, (1, 128), 1)
+    high = lane >= LAT
+    own_half = high.astype(jnp.int32) == core
+
+    def wide(block):
+        return jnp.where(own_half, jnp.concatenate([block, block], axis=-1), 0.0).astype(BF16)
+
+    conv_wide = wide(conv_ref[...])
+    point_wide = wide(point_ref[...].T)
+    for half in range(2):
+        part = slice(half * 16, half * 16 + 16)
+        wsend[half, 0:9] = conv_wide[:, part]
+        wsend[half, 9] = point_wide[part]
+
+    barrier = pltpu.get_barrier_semaphore()
+    partners = [core_peer, (dp, 3 - chan)]
+    partners += [xy_peer(k) for k in (1, 2, 3)] + [z_peer(k) for k in (1, 2, 3)]
+    for partner in partners:
+        pl.semaphore_signal(barrier, inc=1, device_id=partner, device_id_type=MESH)
+    pl.semaphore_wait(barrier, len(partners))
+
+    pre = send(wsend.at[1 - core], wpre, ag_s.at[0, 0], ag_r.at[0, 0], core_peer)
+
+    def halo_copies(up_src, up_dst, down_src, down_dst, at):
+        up = pltpu.make_async_remote_copy(
+            src_ref=up_src, dst_ref=up_dst, send_sem=halo_s.at[at], recv_sem=halo_r.at[at],
+            device_id=up_peer, device_id_type=MESH,
+        )
+        down = pltpu.make_async_remote_copy(
+            src_ref=down_src, dst_ref=down_dst, send_sem=halo_s.at[at + 1], recv_sem=halo_r.at[at + 1],
+            device_id=down_peer, device_id_type=MESH,
+        )
+        return up, down
+
+    def halo_start(copies):
+        @pl.when(chan > 0)
+        def _():
+            copies[0].start()
+
+        @pl.when(chan < 3)
+        def _():
+            copies[1].start()
+
+    def halo_wait_send(copies):
+        @pl.when(chan > 0)
+        def _():
+            copies[0].wait_send()
+
+        @pl.when(chan < 3)
+        def _():
+            copies[1].wait_send()
+
+    def halo_wait_recv(copies):
+        @pl.when(chan < 3)
+        def _():
+            copies[0].wait_recv()
+
+        @pl.when(chan > 0)
+        def _():
+            copies[1].wait_recv()
+
+    cols = pl.ds(0, SIDE)
+    x_halo = halo_copies(
+        x_hbm.at[0, :, cols, :], xhalo.at[1], x_hbm.at[rows - 1, :, cols, :], xhalo.at[0], 0
+    )
+    halo_start(x_halo)
+
+    @pl.when(chan == 0)
+    def _():
+        xhalo[0] = jnp.zeros(xhalo.shape[1:], BF16)
+
+    @pl.when(chan == 3)
+    def _():
+        xhalo[1] = jnp.zeros(xhalo.shape[1:], BF16)
+
+    def gather_buffer(p):
+        return pb if p == 0 else wb.at[p - 1]
+
+    def gather_z(p):
+        buffer = gather_buffer(p)
+        block = buffer.at[core, xc, yc, zc]
+        return [send(block, block, ag_s.at[p, k], ag_r.at[p, k], z_peer(k)) for k in (1, 2, 3)]
+
+    def gather_xy(p):
+        block = gather_buffer(p).at[core, xc, yc]
+        return [send(block, block, ag_s.at[p, 3 + k], ag_r.at[p, 3 + k], xy_peer(k)) for k in (1, 2, 3)]
+
+    def gather_core(p):
+        block = gather_buffer(p).at[core]
+        return [send(block, block, ag_s.at[p, 7], ag_r.at[p, 7], core_peer)]
+
+    def landed(copies):
+        for copy in copies:
+            copy.wait_recv()
+
+    top = mask_ref[0:8, :].astype(F32).T
+    for t in range(BANDS):
+        col_mask[t] = jnp.broadcast_to(top[0:SIDE, t : t + 1], (SIDE, 128))
+    step_in = lax.broadcasted_iota(jnp.int32, (SIDE, 128), 0)
+    not_first = (step_in > 0).astype(F32)
+    not_last = (step_in < SIDE - 1).astype(F32)
+
+    def two(block):
+        return jnp.concatenate([block, block], axis=1)
+
+    def shift_row(block_of, row_flags, at, keep):
+        for t in range(BANDS):
+            valid = col_mask[t] * row_flags[t : t + 1, 0:1]
+            base = aligned(at + t * SIDE, 16)
+            act = jnp.maximum(block_of(t).astype(F32), 0.0) * two(valid)
+            shifted[pl.ds(base, SIDE), 256:512] = act.astype(BF16)
+            before = pltpu.roll(act, 1, 0) * two(not_first)
+            shifted[pl.ds(base, SIDE), 0:256] = before.astype(BF16)
+            after = pltpu.roll(act, SIDE - 1, 0) * two(not_last)
+            shifted[pl.ds(base, SIDE), 512:768] = after.astype(BF16)
+            if keep is not None:
+                mask_rows[pl.ds(aligned(keep + t * SIDE, 16), SIDE), :] = valid.astype(BF16)
+
+    def shift_chunk(k, carry):
+        flags = mask_ref[pl.ds(aligned((chan * rows + k * CHUNK_ROWS) * BANDS, 8), 8), :].astype(F32)
+        for r in range(CHUNK_ROWS):
+            row = k * CHUNK_ROWS + r
+            shift_row(
+                lambda t: xv[row, t],
+                flags[r * BANDS : (r + 1) * BANDS],
+                (row + 1) * PITCH,
+                row * PITCH,
+            )
+        return carry
+
+    x_copy(0).wait()
+    shift_chunk(0, 0)
+    pre.wait_recv()
+    joined = wsend[core] + wpre[...]
+    for i in range(3):
+        wb[i, core, xc, yc, zc] = joined[3 * i : 3 * i + 3]
+    pb[core, xc, yc, zc, 0] = joined[9]
+    quant = jnp.concatenate(
+        [
+            jnp.concatenate([dec_ref[...], proj_ref[...]], axis=1),
+            jnp.concatenate([book_ref[0:8, :], book_ref[8:16, :]], axis=1),
+        ],
+        axis=0,
+    )
+    pb[core, xc, yc, zc, 1] = quant.astype(BF16)
+    on_z = [gather_z(p) for p in range(4)]
+
+    for k in range(1, chunks):
+        x_copy(k).wait()
+    lax.fori_loop(1, chunks, shift_chunk, 0)
+    landed(on_z[0])
+    on_xy = [gather_xy(0)]
+    halo_wait_recv(x_halo)
+
+    def halo_row(side, at, global_row, present):
+        first = aligned(lax.div(jnp.maximum(global_row, 0), 4) * 8, 8)
+        group = mask_ref[pl.ds(first, 8), :].astype(F32)
+        inside = 2 * (3 if side == 0 else 0)
+        flags = group[inside : inside + 2]
+        scale = present.astype(F32)
+
+        shift_row(lambda t: xhalo[side, t], flags * scale, at, None)
+
+    halo_row(0, 0, chan * rows - 1, chan > 0)
+    halo_row(1, (rows + 1) * PITCH, jnp.minimum(chan * rows + rows, 3 * rows), chan < 3)
+
+    landed(on_z[1])
+    on_xy.append(gather_xy(1))
+    landed(on_z[2])
+    on_xy.append(gather_xy(2))
+    landed(on_z[3])
+    on_xy.append(gather_xy(3))
+
+    dec_acc[...] = jnp.zeros_like(dec_acc)
+    proj_acc[...] = jnp.zeros_like(proj_acc)
+    point_acc[...] = jnp.zeros_like(point_acc)
+    book_acc[...] = jnp.zeros_like(book_acc)
+    loss_acc[...] = jnp.zeros_like(loss_acc)
+
+    landed(on_xy[0])
+    on_core = [gather_core(0)]
+    landed(on_core[0])
+
+    blocks = [(h, x, y, z) for z in range(4) for y in range(2) for x in range(2) for h in range(2)]
+    for h, x, y, z in blocks:
+        point_t[z * 64 + y * 32 + h * 16 : z * 64 + y * 32 + h * 16 + 16, x * 128 : x * 128 + 128] = pb[h, x, y, z, 0]
+        owner = (2 * z + y) * 4 + 2 * x + h
+        small = pb[h, x, y, z, 1].astype(F32)
+        qf[owner * 8 : owner * 8 + 8, :] = small[0:8]
+        bookf[owner * 16 : owner * 16 + 8, :] = pltpu.roll(small[8:16], LAT, 1)
+        bookf[owner * 16 + 8 : owner * 16 + 16, :] = small[8:16]
+    point_n[...] = point_t[...].T
+    small = qf[...]
+    decz[...] = jnp.where(high, 0.0, small).astype(BF16)
+    projz[...] = jnp.where(high, small, 0.0).astype(BF16)
+    dz_ref[...] = jnp.where(high, pltpu.roll(small, LAT, 1), 0.0).astype(BF16)
+    proj_t[...] = jnp.where(high, 0.0, pltpu.roll(small, LAT, 1)).astype(BF16).T
+    book_t[...] = jnp.where(high, bookf[...], 0.0).astype(BF16).T
+
+    def onehot_t(k):
+        entries = lax.broadcasted_iota(jnp.int32, (book_t.shape[1], CHUNK), 0)
+        return (entries == ids_ref[k]).astype(F32).astype(BF16)
+
+    def chunk_of(ref, k):
+        return ref[pl.ds(aligned(k * CHUNK, 16), CHUNK), :]
+
+    def pixels_of(ref, k):
+        return ref[pl.ds(k * CHUNK_ROWS, CHUNK_ROWS)].reshape(CHUNK, 256)
+
+    def decoder_chunk(k, carry):
+        valid = chunk_of(mask_rows, k).astype(F32)
+        kept = (pixels_of(cotv, k).astype(F32) * two(valid)).astype(BF16)
+        chosen = dot(book_t[...], onehot_t(k)).T
+        both = chosen + dot(kept, decz[...])
+        u_rows[pl.ds(aligned(k * CHUNK, 16), CHUNK), :] = both
+        both_low = both.astype(BF16)
+        ub_rows[pl.ds(aligned(k * CHUNK, 16), CHUNK), :] = both_low
+        dec_acc[...] += dot_rows(kept, both_low)
+        return carry
+
+    for k in range(chunks):
+        cot_copy(k).wait()
+    lax.fori_loop(0, 2, decoder_chunk, 0)
+    landed(on_xy[1])
+    on_core.append(gather_core(1))
+    lax.fori_loop(2, 4, decoder_chunk, 0)
+    landed(on_xy[2])
+    on_core.append(gather_core(2))
+    lax.fori_loop(4, 6, decoder_chunk, 0)
+    landed(on_xy[3])
+    on_core.append(gather_core(3))
+    lax.fori_loop(6, chunks, decoder_chunk, 0)
+    ub_copy = pltpu.make_async_copy(ub_rows, ub_hbm, ub_sem)
+    ub_copy.start()
+
+    for i in range(3):
+        landed(on_core[1 + i])
+        for h, x, y, z in blocks:
+            for j in range(3):
+                first = j * 256 + z * 64 + y * 32 + h * 16
+                wfull[i, first : first + 16, x * 128 : x * 128 + 128] = wb[i, h, x, y, z, j]
+        for j in range(3):
+            wback[i, :, j * 256 : j * 256 + 256] = wfull[i, j * 256 : j * 256 + 256, :].T
+
+    def forward_chunk(k, carry):
+        hidden = None
+        for i in range(3):
+            window = shifted[pl.ds(aligned((k * CHUNK_ROWS + i) * PITCH, 16), CHUNK), :]
+            term = dot(window, wfull[i])
+            hidden = term if hidden is None else hidden + term
+        middle = jnp.maximum(hidden, 0.0).astype(BF16)
+        branch = dot(middle, point_n[...])
+        summed = (pixels_of(xv, k).astype(F32) + branch).astype(BF16)
+        valid = chunk_of(mask_rows, k).astype(F32)
+        gap = chunk_of(u_rows, k) - dot(summed, projz[...])
+        weighted = gap * valid
+        loss_acc[...] += jnp.sum((weighted * gap).reshape(CHUNK // 8, 8, 128), axis=0)
+        latent_grad = (gap - 0.5 * pltpu.roll(weighted, LAT, 1)).astype(BF16)
+        lg_rows[pl.ds(aligned(k * CHUNK, 16), CHUNK), :] = latent_grad
+        term = 2.0 * weighted
+        coarse = term.astype(BF16).astype(F32)
+        fine = pltpu.roll(term - coarse, LAT, 1)
+        parts = jnp.where(high, coarse, fine).astype(BF16)
+        book_acc[...] += dot(onehot_t(k), parts)
+        proj_acc[...] += dot_rows(summed, latent_grad)
+        resid_low = dot(latent_grad, proj_t[...]).astype(BF16)
+        point_acc[...] += dot_rows(resid_low, middle)
+        back = dot(resid_low, point_t[...])
+        hidden_grad = jnp.where(hidden > 0.0, back, 0.0).astype(BF16)
+        hgp[pl.ds(aligned((k * CHUNK_ROWS + 1) * PITCH, 16), CHUNK), :] = hidden_grad
+        hgt[:, pl.ds(aligned(k * CHUNK, 128), CHUNK)] = hidden_grad.T
+        return carry
+
+    lax.fori_loop(0, chunks, forward_chunk, 0)
+
+    zero_row = jnp.zeros((PITCH, 256), BF16)
+
+    @pl.when(chan == 0)
+    def _():
+        hgp[0:PITCH, :] = zero_row
+
+    @pl.when(chan == 3)
+    def _():
+        hgp[(rows + 1) * PITCH : (rows + 2) * PITCH, :] = zero_row
+
+    def grad_row(r):
+        return hgp.at[pl.ds(r * PITCH, PITCH), :]
+
+    hg_halo = halo_copies(grad_row(1), grad_row(rows + 1), grad_row(rows), grad_row(0), 2)
+    halo_start(hg_halo)
+
+    def reduce_buffers(p):
+        if p == 0:
+            return gp, rp0, rp1, rp2
+        return gs.at[p - 1], rc0.at[p - 1], rc1.at[p - 1], rc2.at[p - 1]
+
+    def reduce_core(p):
+        buffer, first, _, _ = reduce_buffers(p)
+        return [send(buffer.at[1 - core], first, rs_s.at[p, 0], rs_r.at[p, 0], core_peer)]
+
+    def reduce_xy(p, copies):
+        landed(copies)
+        buffer, first, second, _ = reduce_buffers(p)
+        buffer[core] = buffer[core] + first[...]
+        out = []
+        for k in (1, 2, 3):
+            x_new, y_new = xy_of(k)
+            out.append(
+                send(buffer.at[core, x_new, y_new], second.at[k - 1], rs_s.at[p, k], rs_r.at[p, k], xy_peer(k))
+            )
+        return out
+
+    def reduce_z(p, copies):
+        landed(copies)
+        buffer, _, second, third = reduce_buffers(p)
+        buffer[core, xc, yc] = (buffer[core, xc, yc] + second[0]) + (second[1] + second[2])
+        return [
+            send(buffer.at[core, xc, yc, z_of(k)], third.at[k - 1], rs_s.at[p, 3 + k], rs_r.at[p, 3 + k], z_peer(k))
+            for k in (1, 2, 3)
+        ]
+
+    def reduce_end(p, copies):
+        landed(copies)
+        buffer, _, _, third = reduce_buffers(p)
+        total = (buffer[core, xc, yc, zc] + third[0]) + (third[1] + third[2])
+        if p == 0:
+            q_ref[...] = total[16:40]
+            fin[9] = total[0:16]
+        else:
+            for j in range(3):
+                fin[3 * (p - 1) + j] = total[j * 16 : j * 16 + 16]
+
+    counts = mask_ref[pl.ds(aligned(chan * rows * BANDS, 8), rows * BANDS), :].astype(F32)
+    counts = jnp.sum(counts.reshape(rows * BANDS // 8, 8, 128), axis=0)
+    tallies = jnp.where(high, loss_acc[...], counts + pltpu.roll(counts, LAT, 1))
+    heads = jnp.where(high, dec_acc[...], proj_acc[...])
+    book_sum = book_acc[...] + pltpu.roll(book_acc[...], LAT, 1)
+    for h, x, y, z in blocks:
+        first = z * 64 + y * 32 + h * 16
+        owner = (2 * z + y) * 4 + 2 * x + h
+        gp[h, x, y, z, 0:16] = point_acc[first : first + 16, x * 128 : x * 128 + 128]
+        gp[h, x, y, z, 16:24] = heads[owner * 8 : owner * 8 + 8]
+        gp[h, x, y, z, 24:32] = jnp.where(
+            high, book_sum[owner * 16 + 8 : owner * 16 + 16], book_sum[owner * 16 : owner * 16 + 8]
+        )
+        gp[h, x, y, z, 32:40] = tallies
+    stage = [reduce_core(0), None, None, None]
+
+    def conv_grad(i):
+        product = dot(hgt[...], shifted[i * PITCH : i * PITCH + pixels, :])
+        for j in range(3):
+            turned = product[:, j * 256 : j * 256 + 256].T
+            for h, x, y, z in blocks:
+                first = z * 64 + y * 32 + h * 16
+                gs[i, h, x, y, z, j * 16 : j * 16 + 16] = turned[first : first + 16, x * 128 : x * 128 + 128]
+
+    conv_grad(0)
+    stage[1] = reduce_core(1)
+    stage[0] = reduce_xy(0, stage[0])
+    conv_grad(1)
+    stage[2] = reduce_core(2)
+    stage[1] = reduce_xy(1, stage[1])
+    conv_grad(2)
+    stage[3] = reduce_core(3)
+    stage[2] = reduce_xy(2, stage[2])
+    stage[0] = reduce_z(0, stage[0])
+    halo_wait_recv(hg_halo)
+
+    edge_first = two(not_first)[None]
+    edge_last = two(not_last)[None]
+
+    def out_copy(k):
+        part = pl.ds(k * CHUNK_ROWS, CHUNK_ROWS)
+        return pltpu.make_async_copy(cotv.at[part], ig_hbm.at[part], out_sem.at[k])
+
+    def back_chunk(k, carry):
+        total = None
+        for i in range(3):
+            window = hgp[pl.ds(aligned((k * CHUNK_ROWS + 2 - i) * PITCH, 16), CHUNK), :]
+            term = dot(window, wback[i])
+            total = term if total is None else total + term
+        segments = CHUNK // SIDE
+        before = pltpu.roll(total[:, 512:768], 1, 0).reshape(segments, SIDE, 256) * edge_first
+        after = pltpu.roll(total[:, 0:256], CHUNK - 1, 0).reshape(segments, SIDE, 256) * edge_last
+        back_grad = total[:, 256:512] + (before + after).reshape(CHUNK, 256)
+        slope = shifted[pl.ds(aligned((k * CHUNK_ROWS + 1) * PITCH, 16), CHUNK), 256:512].astype(F32) > 0.0
+        resid = dot(chunk_of(lg_rows, k), proj_t[...])
+        grad = (resid + jnp.where(slope, back_grad, 0.0)).astype(BF16)
+        cotv[pl.ds(k * CHUNK_ROWS, CHUNK_ROWS)] = grad.reshape(CHUNK_ROWS, BANDS, SIDE, 256)
+        return carry
+
+    def back_chunks(first, last):
+        lax.fori_loop(first, last, back_chunk, 0)
+        for k in range(first, last):
+            out_copy(k).start()
+
+    back_chunks(0, 1)
+    stage[3] = reduce_xy(3, stage[3])
+    back_chunks(1, 3)
+    stage[1] = reduce_z(1, stage[1])
+    reduce_end(0, stage[0])
+    back_chunks(3, 5)
+    stage[2] = reduce_z(2, stage[2])
+    reduce_end(1, stage[1])
+    back_chunks(5, chunks)
+    stage[3] = reduce_z(3, stage[3])
+    reduce_end(2, stage[2])
+    reduce_end(3, stage[3])
+    last = send(fin, rx3, rs_s.at[0, 7], rs_r.at[0, 7], core_peer)
+    last.wait_recv()
+    mine, other = fin[...], rx3[...]
+    is_first = core == 0
+    lower = jnp.where(is_first, mine, other)
+    upper = jnp.where(is_first, other, mine)
+    whole = jnp.concatenate([lower, upper], axis=1)
+    g_ref[...] = jnp.where(is_first, whole[..., 0:LAT], whole[..., LAT:])
+
+    for k in range(chunks):
+        out_copy(k).wait()
+    ub_copy.wait()
+    halo_wait_send(x_halo)
+    halo_wait_send(hg_halo)
+    for copy in pending:
+        copy.wait_send()
+
+
+def finish_kernel(
+    ig_ref, ub_ref, mask_ref, dec_ref, g_ref, q_ref,
+    conv_w, conv_m, conv_v, point_w, point_m, point_v, proj_w, proj_m, proj_v,
+    code_w, code_m, code_v, dec_w, dec_m, dec_v,
+    out_ref, grad_ref, loss_ref, *updates,
+):
+    step = pl.program_id(0)
+    steps_rows = out_ref.shape[0]
+    chan = lax.axis_index("chan")
+    first = (chan * pl.num_programs(0) + step) * steps_rows * BANDS
+    flags = mask_ref[pl.ds(aligned(first, 8), steps_rows * BANDS), :].astype(F32)
+    top = mask_ref[0:8, :].astype(F32).T
+    decoded = lax.dot_general(
+        ub_ref[...], dec_ref[...], (((1,), (1,)), ((), ())), preferred_element_type=F32
+    )
+    decoded = decoded.reshape(steps_rows, BANDS, SIDE, 256)
+    for r in range(steps_rows):
+        for t in range(BANDS):
+            at = r * BANDS + t
+            valid = top[0:SIDE, t : t + 1] * flags[at : at + 1, 0:1]
+            out_ref[r, t, 0:SIDE, :] = (decoded[r, t] * valid).astype(BF16)
+            grad_ref[r, t, 0:SIDE, :] = ig_ref[r, t]
+
+    @pl.when(step == 0)
+    def _():
+        q = q_ref[...]
+        heads, book = q[0:8], q[8:16]
+        high = lax.broadcasted_iota(jnp.int32, (8, 128), 1) >= LAT
+        gap = jnp.sum(jnp.where(high, q[16:24], 0.0))
+        count = jnp.sum(jnp.where(high, 0.0, q[16:24]))
+        ratio = jnp.full((8, 128), gap, F32) / jnp.full((8, 128), count * LAT, F32)
+        row = lax.broadcasted_iota(jnp.int32, (8, 128), 0)
+        loss_ref[...] = jnp.where(row == 0, ratio, 0.25 * ratio)
+        sets = (
+            (g_ref[0:9], conv_w, conv_m, conv_v, 0.01),
+            (g_ref[9].T, point_w, point_m, point_v, 0.03),
+            (heads[:, 0:LAT], proj_w, proj_m, proj_v, 0.03),
+            (jnp.concatenate([book[:, 0:LAT], book[:, LAT:]], axis=0), code_w, code_m, code_v, 0.5),
+            (heads[:, LAT:], dec_w, dec_m, dec_v, 0.06),
+        )
+        for n, (grad, weight, moment, square, rate) in enumerate(sets):
+            results = adamw(grad, weight[...], moment[...], square[...], rate)
+            for m in range(4):
+                updates[4 * n + m][...] = results[m]
+
+
+def vmem():
+    return pl.BlockSpec(memory_space=pltpu.VMEM)
+
+
+def anywhere():
+    return pl.BlockSpec(memory_space=pl.ANY)
+
+
+def on_device(
+    inputs, valid_mask, code_ids, cotangent,
+    conv_weight, conv_first, conv_second, point_weight, point_first, point_second,
+    proj_weight, proj_first, proj_second, code_book, code_first, code_second,
+    dec_weight, dec_first, dec_second,
+):
+    channels = inputs.shape[1]
+    rows = inputs.shape[0] // (BANDS * BAND)
+    chunks = rows // CHUNK_ROWS
+    pixels = rows * PITCH
+    padded = pixels + 2 * PITCH
+    entries = 32 * code_book.shape[0]
+    canvas = (rows, BANDS, BAND, channels)
+    mask = valid_mask.reshape(-1, BAND)
+    ids = code_ids.reshape(rows * BANDS, BAND)[:, :SIDE].reshape(chunks, 1, CHUNK)
+    packed = (rows, BANDS, SIDE, channels)
+    dma = pltpu.SemaphoreType.DMA
+    ub, ig, grads, quant, decoder = pl.pallas_call(
+        functools.partial(block_kernel, rows),
+        out_shape=(
+            jax.ShapeDtypeStruct((pixels, 128), BF16),
+            jax.ShapeDtypeStruct(packed, BF16),
+            jax.ShapeDtypeStruct((10, 32, LAT), F32),
+            jax.ShapeDtypeStruct((24, 128), F32),
+            jax.ShapeDtypeStruct((channels, 128), BF16),
+        ),
+        in_specs=[anywhere()] * 2 + [vmem()] * 7,
+        out_specs=(anywhere(), anywhere(), vmem(), vmem(), vmem()),
+        scratch_shapes=[
+            pltpu.VMEM(packed, BF16),
+            pltpu.VMEM((2, BANDS, SIDE, channels), BF16),
+            pltpu.VMEM(packed, BF16),
+            pltpu.VMEM((padded, 3 * channels), BF16),
+            pltpu.VMEM((pixels, 128), BF16),
+            pltpu.VMEM((BANDS, SIDE, 128), F32),
+            pltpu.VMEM((pixels, 128), F32),
+            pltpu.VMEM((pixels, 128), BF16),
+            pltpu.VMEM((pixels, 128), BF16),
+            pltpu.VMEM((padded, channels), BF16),
+            pltpu.VMEM((channels, pixels), BF16),
+            pltpu.VMEM((2, 10, 16, 128), BF16),
+            pltpu.VMEM((10, 16, 128), BF16),
+            pltpu.VMEM((3, 2, 2, 2, 4, 3, 16, 128), BF16),
+            pltpu.VMEM((2, 2, 2, 4, 2, 16, 128), BF16),
+            pltpu.VMEM((3, 3 * channels, channels), BF16),
+            pltpu.VMEM((3, channels, 3 * channels), BF16),
+            pltpu.VMEM((channels, channels), BF16),
+            pltpu.VMEM((channels, channels), BF16),
+            pltpu.VMEM((channels, 128), F32),
+            pltpu.VMEM((entries, 128), F32),
+            pltpu.VMEM((channels, 128), BF16),
+            pltpu.VMEM((channels, 128), BF16),
+            pltpu.VMEM((128, channels), BF16),
+            pltpu.VMEM((128, entries), BF16),
+            pltpu.VMEM((channels, 128), F32),
+            pltpu.VMEM((channels, 128), F32),
+            pltpu.VMEM((channels, channels), F32),
+            pltpu.VMEM((entries, 128), F32),
+            pltpu.VMEM((8, 128), F32),
+            pltpu.VMEM((2, 2, 2, 4, 40, 128), F32),
+            pltpu.VMEM((3, 2, 2, 2, 4, 48, 128), F32),
+            pltpu.VMEM((2, 2, 4, 40, 128), F32),
+            pltpu.VMEM((3, 4, 40, 128), F32),
+            pltpu.VMEM((3, 40, 128), F32),
+            pltpu.VMEM((3, 2, 2, 4, 48, 128), F32),
+            pltpu.VMEM((3, 3, 4, 48, 128), F32),
+            pltpu.VMEM((3, 3, 48, 128), F32),
+            pltpu.VMEM((10, 16, 128), F32),
+            pltpu.VMEM((10, 16, 128), F32),
+            dma((chunks,)),
+            dma((chunks,)),
+            dma((chunks,)),
+            dma(()),
+            dma((4,)),
+            dma((4,)),
+            dma((4, 8)),
+            dma((4, 8)),
+            dma((4, 8)),
+            dma((4, 8)),
+        ],
+        compiler_params=pltpu.CompilerParams(
+            collective_id=0, has_side_effects=True, vmem_limit_bytes=60 * 2**20
+        ),
+        name="block",
+    )(
+        inputs.reshape(canvas), cotangent.reshape(canvas), ids, mask,
+        conv_weight, point_weight, proj_weight, code_book, dec_weight,
+    )
+
+    states = (
+        conv_weight, conv_first, conv_second, point_weight, point_first, point_second,
+        proj_weight, proj_first, proj_second, code_book, code_first, code_second,
+        dec_weight, dec_first, dec_second,
+    )
+    tiles = pl.BlockSpec((CHUNK_ROWS, BANDS, BAND, channels), lambda n: (n, 0, 0, 0))
+
+    def whole(shape):
+        return pl.BlockSpec(shape, lambda n: (0,) * len(shape))
+
+    updates, specs = [], []
+    for n in range(5):
+        shape = states[3 * n].shape
+        for kind in (F32, F32, F32, BF16):
+            updates.append(jax.ShapeDtypeStruct(shape, kind))
+            specs.append(whole(shape))
+    results = pl.pallas_call(
+        finish_kernel,
+        grid=(chunks,),
+        out_shape=(
+            jax.ShapeDtypeStruct(canvas, BF16),
+            jax.ShapeDtypeStruct(canvas, BF16),
+            jax.ShapeDtypeStruct((8, 128), F32),
+            *updates,
+        ),
+        in_specs=[
+            pl.BlockSpec((CHUNK_ROWS, BANDS, SIDE, channels), lambda n: (n, 0, 0, 0)),
+            pl.BlockSpec((CHUNK, 128), lambda n: (n, 0)),
+            whole(mask.shape),
+            whole(decoder.shape),
+            whole(grads.shape),
+            whole(quant.shape),
+            *[whole(s.shape) for s in states],
+        ],
+        out_specs=(tiles, tiles, whole((8, 128)), *specs),
+        compiler_params=pltpu.CompilerParams(vmem_limit_bytes=40 * 2**20),
+        name="finish",
+    )(ig, ub, mask, decoder, grads, quant, *states)
+    output, input_grad, ratio = results[:3]
+    return (
+        output.reshape(inputs.shape),
+        input_grad.reshape(inputs.shape),
+        ratio[0:2, 0],
+        *results[3:],
+    )
 
 
 def row_stride():
@@ -97,18 +863,7 @@
     return (output, latent_grad, decoder_grad, book_grad, loss_part, count_part)
 
 
-def adamw(grad, weight, first, second, rate):
-    first_new = beta_first * first + (1.0 - beta_first) * grad
-    second_new = beta_second * second + (1.0 - beta_second) * grad * grad
-    first_hat = first_new / (1.0 - beta_first**STEP)
-    second_hat = second_new / (1.0 - beta_second**STEP)
-    weight_new = weight - rate * (
-        first_hat / (jnp.sqrt(second_hat) + epsilon) + decay_rate * weight
-    )
-    return (weight_new, first_new, second_new, weight_new.astype(jnp.bfloat16))
-
-
-def on_device(
+def general(
     inputs,
     valid_mask,
     code_ids,
@@ -243,52 +998,11 @@
 
 
 def solution(mesh):
-    in_specs = (
-        P(("dp", "chan"), None),
-        P("dp"),
-        P(("dp", "chan")),
-        P(("dp", "chan"), None),
-        P(None, "dp", "chan"),
-        P(None, "dp", "chan"),
-        P(None, "dp", "chan"),
-        P("chan", "dp"),
-        P("chan", "dp"),
-        P("chan", "dp"),
-        P(("dp", "chan"), None),
-        P(("dp", "chan"), None),
-        P(("dp", "chan"), None),
-        P(("dp", "chan"), None),
-        P(("dp", "chan"), None),
-        P(("dp", "chan"), None),
-        P(("dp", "chan"), None),
-        P(("dp", "chan"), None),
-        P(("dp", "chan"), None),
-    )
-    out_specs = (
-        P(("dp", "chan"), None),
-        P(("dp", "chan"), None),
-        P(),
-        P(None, "dp", "chan"),
-        P(None, "dp", "chan"),
-        P(None, "dp", "chan"),
-        P(None, "dp", "chan"),
-        P("chan", "dp"),
-        P("chan", "dp"),
-        P("chan", "dp"),
-        P("chan", "dp"),
-        P(("dp", "chan"), None),
-        P(("dp", "chan"), None),
-        P(("dp", "chan"), None),
-        P(("dp", "chan"), None),
-        P(("dp", "chan"), None),
-        P(("dp", "chan"), None),
-        P(("dp", "chan"), None),
-        P(("dp", "chan"), None),
-        P(("dp", "chan"), None),
-        P(("dp", "chan"), None),
-        P(("dp", "chan"), None),
-        P(("dp", "chan"), None),
-    )
-    return jax.shard_map(
-        on_device, mesh=mesh, in_specs=in_specs, out_specs=out_specs, check_vma=False
-    )
+    pixel = P(("dp", "chan"), None)
+    conv, point = P(None, "dp", "chan"), P("chan", "dp")
+    in_specs = (pixel, P("dp"), P(("dp", "chan")), pixel)
+    in_specs += (conv,) * 3 + (point,) * 3 + (pixel,) * 9
+    out_specs = (pixel, pixel, P()) + (conv,) * 4 + (point,) * 4 + (pixel,) * 12
+    fits = mesh.shape["dp"] == 8 and mesh.shape["chan"] == 4
+    body = on_device if fits else general
+    return jax.shard_map(body, mesh=mesh, in_specs=in_specs, out_specs=out_specs, check_vma=False)

time: 1420 us -> 118 us (0.08)
  waiting for transfers between devices: 613 us -> 0 us
  matrix products: 491 us -> 0 us
  blocking collectives: 223 us -> 0 us
  Pallas kernels: 0 us -> 104 us
  other arithmetic: 33 us -> 0 us
  local copies, waits for them, and re-layouts: 29.2 us -> 12.7 us
  between operations: 16.3 us -> 0.91 us
    dot_general x38 -> x0, matrix products: 491 us -> none  [the longest x9 220 us: conv_input_grad(): lax.dot_general(window, weights[tap_index], (((1,), (1,)), ((), ())), pre...]
    reduce_scatter x6 -> x0, waiting for transfers between devices: 454 us -> none  [the longest x1 235 us: on_device(): lax.psum_scatter(lax.dynamic_update_slice_in_dim(back_grad, own_back + re...]
    all_gather x5 -> x0, blocking collectives: 183 us -> none  [the longest x1 41.1 us: on_device(): lax.all_gather(dec_weight.astype(jnp.bfloat16), ('dp', 'chan'), axis=0, t...]
    all_gather x3 -> x0, waiting for transfers between devices: 159 us -> none  [the longest x1 82 us: on_device(): lax.all_gather(resid.astype(jnp.bfloat16), 'chan', axis=1, tiled=True)]
    pallas_call x0 -> x2, Pallas kernels: none -> 104 us  [the longest x1 97 us: on_device(): pl.pallas_call(functools.partial(block_kernel, rows), out_shape=(jax.Shap...]
    psum x1 -> x0, blocking collectives: 40.3 us -> none  [on_device(): loss_total, count_total = lax.psum((loss_part, count_part), ('dp', 'chan'))]
    unnamed x89 -> x45, local copies, waits for them, and re-layouts: 26.8 us -> 12 us
  transfers between devices with their start and end apart: 10 -> 0, of which waited for: 6 -> 0; matrix products, arithmetic and copies ran while one was open for 27% -> 0% of each run, Pallas kernels for 0% -> 0%
where the time goes in v1:
time: 118 us; the launch traced here: 117 us
  Pallas kernels  104 us (88%)
  local copies, waits for them, and re-layouts  12.7 us (11%)
    pallas_call x1, Pallas kernels, on_device(): pl.pallas_call(functools.partial(block_kernel, rows), out_shape=(jax.Shap...  97 us
    unnamed x45, local copies, waits for them, and re-layouts  12 us
    pallas_call x1, Pallas kernels, on_device(): pl.pallas_call(finish_kernel, grid=(chunks,), out_shape=(jax.ShapeDtypeSt...  6.71 us

profile of v1, /device:TPU:0, one launch (start us, length us, event | category | flops | bytes accessed | tf_op | source)
XLA Modules:
  0.0 117.3 jit_solution(502396992471050309)
XLA Ops:
  0.7 1.4 %copy.50.point_ref.point_w = f32[64,32]{1,0:T(8,128)} copy(f32[64,32]{0,1:T(8,128)} %param.26) | data formatting | bytes 16384 | tf_op args[7]
  2.1 0.8 copy.52.point_m
  2.9 0.8 copy.53.point_v
  3.7 0.0 copy-start.3
  3.7 0.0 copy-start.4
  3.7 0.0 copy-start.6
  3.7 0.0 copy-start.7
  3.7 0.0 copy-start.9
  3.7 0.0 copy-start.10
  3.7 0.0 copy-start.11
  3.8 0.0 copy-start.13
  3.8 0.0 copy-start.14
  3.8 0.0 copy-start.15
  3.8 0.0 copy-start.16
  3.8 0.0 copy-start.17
  3.8 0.0 copy-start.18
  3.8 97.0 %block.1 = (bf16[8192,128]{1,0:T(8,128)(2,1)}, bf16[32,2,128,256]{3,2,1,0:T(8,128)(2,1)}, f32[10,32,64]{2,1,0:T(8,128)}, f32[24,128]{1,0:T(8,128)}, bf16[256,128]{1,0:T(8,128)(2,1)}) custom-call(bf16[32,2,128,256]{3,2,1,0:T(8,128)(2,1)} %bitcast.8, bf16[32,2,128,256]{3,2,1,0:T(8,128)(2,1)} %bitcast.9, s32[8,1,1024]{2,1,0:T(1,128)} %bitcast.10, ...), custom_call_target="tpu_custom_call" | custom-call | tf_op jit(solution)/shard_map/block/pallas_call | solution.py:665
  100.8 0.0 copy-done.2
  100.8 0.0 copy-done.3
  100.9 0.0 copy-done.4
  100.9 0.0 copy-done.6
  101.0 2.2 %copy-done = bf16[32,2,128,256]{3,2,1,0:T(8,128)(2,1)S(1)} copy-done((bf16[32,2,128,256]{3,2,1,0:T(8,128)(2,1)S(1)}, bf16[32,2,128,256]{3,2,1,0:T(8,128)(2,1)}, u32[]{:S(2)}) %copy-start) | copy-done | bytes 4194328
  103.2 1.6 %copy-done.1 = bf16[8192,128]{1,0:T(8,128)(2,1)S(1)} copy-done((bf16[8192,128]{1,0:T(8,128)(2,1)S(1)}, bf16[8192,128]{1,0:T(8,128)(2,1)}, u32[]{:S(2)}) %copy-start.1) | copy-done | bytes 2097176
  104.8 0.9 copy-done.5
  105.7 0.8 copy-done.8
  106.5 0.7 copy-done.12
  107.2 6.7 %finish.1 = (bf16[32,2,128,256]{3,2,1,0:T(8,128)(2,1)}, bf16[32,2,128,256]{3,2,1,0:T(8,128)(2,1)}, f32[8,128]{1,0:T(8,128)S(1)}, f32[9,32,64]{2,1,0:T(8,128)}, f...) custom-call(bf16[32,2,128,256]{3,2,1,0:T(8,128)(2,1)S(1)} %copy-done, ...), custom_call_target="tpu_custom_call" | custom-call | tf_op jit(solution)/shard_map/finish/pallas_call | solution.py:753
  113.9 0.6 slice_reduce_fusion
  114.6 0.7 copy.57
  115.2 0.7 copy.54
  115.9 0.7 copy.55
  116.6 0.7 copy.56
  (16 shorter events, 0.0 us)
Async XLA Ops:
  3.7 97.2 %copy-start.2 = (f32[9,32,64]{2,1,0:T(8,128)S(1)}, f32[9,32,64]{2,1,0:T(8,128)}, u32[]{:S(2)}) copy-start(f32[9,32,64]{2,1,0:T(8,128)} %conv_w.1) | copy-start | bytes 221188
  3.7 97.2 %copy-start.3 = (s32[32768]{0:T(1024)S(1)}, s32[32768]{0:T(1024)}, u32[]{:S(2)}) copy-start(s32[32768]{0:T(1024)} %param.20) | copy-start | bytes 393220
  3.7 97.2 %copy-start.4 = (f32[64,32]{1,0:T(8,128)S(1)}, f32[64,32]{1,0:T(8,128)}, u32[]{:S(2)}) copy-start(f32[64,32]{1,0:T(8,128)} %copy.50.point_ref.point_w) | copy-start | bytes 24580
  3.7 97.2 %copy-start.6 = (f32[9,32,64]{2,1,0:T(8,128)S(1)}, f32[9,32,64]{2,1,0:T(8,128)}, u32[]{:S(2)}) copy-start(f32[9,32,64]{2,1,0:T(8,128)} %conv_m.1) | copy-start | bytes 221188
  3.7 97.2 %copy-start.7 = (f32[9,32,64]{2,1,0:T(8,128)S(1)}, f32[9,32,64]{2,1,0:T(8,128)}, u32[]{:S(2)}) copy-start(f32[9,32,64]{2,1,0:T(8,128)} %conv_v.1) | copy-start | bytes 221188
  3.7 97.2 %copy-start.9 = (f32[16,64]{1,0:T(8,128)S(1)}, f32[16,64]{1,0:T(8,128)}, u32[]{:S(2)}) copy-start(f32[16,64]{1,0:T(8,128)} %code_w.1) | copy-start | bytes 12292
  3.7 97.2 %copy-start.10 = (f32[8,64]{1,0:T(8,128)S(1)}, f32[8,64]{1,0:T(8,128)}, u32[]{:S(2)}) copy-start(f32[8,64]{1,0:T(8,128)} %proj_w.1) | copy-start | bytes 6148
  3.7 97.2 %copy-start.11 = (f32[8,64]{1,0:T(8,128)S(1)}, f32[8,64]{1,0:T(8,128)}, u32[]{:S(2)}) copy-start(f32[8,64]{1,0:T(8,128)} %dec_w.1) | copy-start | bytes 6148
  3.8 97.2 %copy-start.13 = (f32[16,64]{1,0:T(8,128)S(1)}, f32[16,64]{1,0:T(8,128)}, u32[]{:S(2)}) copy-start(f32[16,64]{1,0:T(8,128)} %code_m.1) | copy-start | bytes 12292
  3.8 97.2 %copy-start.14 = (f32[16,64]{1,0:T(8,128)S(1)}, f32[16,64]{1,0:T(8,128)}, u32[]{:S(2)}) copy-start(f32[16,64]{1,0:T(8,128)} %code_v.1) | copy-start | bytes 12292
  3.8 97.2 %copy-start.15 = (f32[8,64]{1,0:T(8,128)S(1)}, f32[8,64]{1,0:T(8,128)}, u32[]{:S(2)}) copy-start(f32[8,64]{1,0:T(8,128)} %proj_m.1) | copy-start | bytes 6148
  3.8 97.1 %copy-start.16 = (f32[8,64]{1,0:T(8,128)S(1)}, f32[8,64]{1,0:T(8,128)}, u32[]{:S(2)}) copy-start(f32[8,64]{1,0:T(8,128)} %proj_v.1) | copy-start | bytes 6148
  3.8 97.1 %copy-start.17 = (f32[8,64]{1,0:T(8,128)S(1)}, f32[8,64]{1,0:T(8,128)}, u32[]{:S(2)}) copy-start(f32[8,64]{1,0:T(8,128)} %dec_m.1) | copy-start | bytes 6148
  3.8 97.1 %copy-start.18 = (f32[8,64]{1,0:T(8,128)S(1)}, f32[8,64]{1,0:T(8,128)}, u32[]{:S(2)}) copy-start(f32[8,64]{1,0:T(8,128)} %dec_v.1) | copy-start | bytes 6148
  101.0 2.2 %copy-start = (bf16[32,2,128,256]{3,2,1,0:T(8,128)(2,1)S(1)}, bf16[32,2,128,256]{3,2,1,0:T(8,128)(2,1)}, u32[]{:S(2)}) copy-start(bf16[32,2,128,256]{3,2,1,0:T(8,128)(2,1)} %get-tuple-element.51.ig_ref) | copy-start | bytes 12582916
  103.2 1.6 %copy-start.1 = (bf16[8192,128]{1,0:T(8,128)(2,1)S(1)}, bf16[8192,128]{1,0:T(8,128)(2,1)}, u32[]{:S(2)}) copy-start(bf16[8192,128]{1,0:T(8,128)(2,1)} %get-tuple-element.52.ub_ref) | copy-start | bytes 6291460
  104.8 0.9 copy-start.5
  105.7 0.8 copy-start.8
  106.5 0.7 copy-start.12

commit v2 on v1

--- a/solution.py
+++ b/solution.py
@@ -11,9 +11,8 @@
 BAND = 128
 BANDS = 2
 STEP = 5
-SIDE = BAND
-PITCH = BANDS * SIDE
-CHUNK_ROWS = 4
+PITCH = BANDS * BAND
+CHUNK_ROWS = 8
 CHUNK = CHUNK_ROWS * PITCH
 MESH = pl.DeviceIdType.MESH
 F32 = jnp.float32
@@ -68,10 +67,8 @@
     xhalo,
     cotv,
     shifted,
-    mask_rows,
     col_mask,
     u_rows,
-    ub_rows,
     lg_rows,
     hgp,
     hgt,
@@ -119,46 +116,39 @@
     core, xc = lax.rem(chan, 2), lax.div(chan, 2)
     yc, zc = lax.rem(dp, 2), lax.div(dp, 2)
     core_peer = (dp, chan + 1 - 2 * core)
-
-    def xy_of(k):
-        x_new = 1 - xc if k % 2 else xc
-        y_new = 1 - yc if k // 2 else yc
-        return x_new, y_new
-
-    def xy_peer(k):
-        x_new, y_new = xy_of(k)
-        return (2 * zc + y_new, 2 * x_new + core)
-
-    def z_of(k):
-        if k == 1:
-            return zc + 1 - 2 * lax.rem(zc, 2)
-        if k == 2:
-            return lax.rem(zc + 2, 4)
-        return 3 - zc
-
-    def z_peer(k):
-        return (2 * z_of(k) + yc, chan)
-
+    other_core = 1 - core
+    xy_of = [(1 - xc if k % 2 else xc, 1 - yc if k // 2 else yc) for k in range(4)]
+    xy_peer = [(2 * zc + y, 2 * x + core) for x, y in xy_of]
+    z_of = [zc, zc + 1 - 2 * lax.rem(zc, 2), lax.rem(zc + 2, 4), 3 - zc]
+    z_peer = [(2 * z + yc, chan) for z in z_of]
     up_peer, down_peer = (dp, chan - 1), (dp, chan + 1)
     chunks = rows // CHUNK_ROWS
     pixels = rows * PITCH
-    pending = []
-
-    def send(src, dst, s_sem, r_sem, peer):
-        copy = pltpu.make_async_remote_copy(
+    def remote(src, dst, s_sem, r_sem, peer):
+        return pltpu.make_async_remote_copy(
             src_ref=src, dst_ref=dst, send_sem=s_sem, recv_sem=r_sem, device_id=peer, device_id_type=MESH
         )
-        copy.start()
-        pending.append(copy)
-        return copy
+
+    def start(copies):
+        for copy in copies:
+            copy.start()
+
+    def landed(copies):
+        for copy in copies:
+            copy.wait_recv()
+
+    def sent(copies):
+        for copy in copies:
+            copy.wait_send()
+
+    def part(k):
+        return pl.ds(k * CHUNK, CHUNK)
 
     def x_copy(k):
-        part = pl.ds(k * CHUNK_ROWS, CHUNK_ROWS)
-        return pltpu.make_async_copy(x_hbm.at[part, :, pl.ds(0, SIDE), :], xv.at[part], x_sem.at[k])
+        return pltpu.make_async_copy(x_hbm.at[part(k)], xv.at[part(k)], x_sem.at[k])
 
     def cot_copy(k):
-        part = pl.ds(k * CHUNK_ROWS, CHUNK_ROWS)
-        return pltpu.make_async_copy(cot_hbm.at[part, :, pl.ds(0, SIDE), :], cotv.at[part], cot_sem.at[k])
+        return pltpu.make_async_copy(cot_hbm.at[part(k)], cotv.at[part(k)], cot_sem.at[k])
 
     for k in range(chunks):
         x_copy(k).start()
@@ -173,30 +163,25 @@
         return jnp.where(own_half, jnp.concatenate([block, block], axis=-1), 0.0).astype(BF16)
 
     conv_wide = wide(conv_ref[...])
-    point_wide = wide(point_ref[...].T)
+    point_wide = wide(point_ref[...])
     for half in range(2):
-        part = slice(half * 16, half * 16 + 16)
-        wsend[half, 0:9] = conv_wide[:, part]
-        wsend[half, 9] = point_wide[part]
+        sixteen = slice(half * 16, half * 16 + 16)
+        wsend[half, 0:9] = conv_wide[:, sixteen]
+        wsend[half, 9] = point_wide[sixteen]
 
     barrier = pltpu.get_barrier_semaphore()
     partners = [core_peer, (dp, 3 - chan)]
-    partners += [xy_peer(k) for k in (1, 2, 3)] + [z_peer(k) for k in (1, 2, 3)]
+    partners += xy_peer[1:] + z_peer[1:]
     for partner in partners:
         pl.semaphore_signal(barrier, inc=1, device_id=partner, device_id_type=MESH)
     pl.semaphore_wait(barrier, len(partners))
 
-    pre = send(wsend.at[1 - core], wpre, ag_s.at[0, 0], ag_r.at[0, 0], core_peer)
+    pre = remote(wsend.at[other_core], wpre, ag_s.at[0, 0], ag_r.at[0, 0], core_peer)
+    pre.start()
 
     def halo_copies(up_src, up_dst, down_src, down_dst, at):
-        up = pltpu.make_async_remote_copy(
-            src_ref=up_src, dst_ref=up_dst, send_sem=halo_s.at[at], recv_sem=halo_r.at[at],
-            device_id=up_peer, device_id_type=MESH,
-        )
-        down = pltpu.make_async_remote_copy(
-            src_ref=down_src, dst_ref=down_dst, send_sem=halo_s.at[at + 1], recv_sem=halo_r.at[at + 1],
-            device_id=down_peer, device_id_type=MESH,
-        )
+        up = remote(up_src, up_dst, halo_s.at[at], halo_r.at[at], up_peer)
+        down = remote(down_src, down_dst, halo_s.at[at + 1], halo_r.at[at + 1], down_peer)
         return up, down
 
     def halo_start(copies):
@@ -226,10 +211,8 @@
         def _():
             copies[1].wait_recv()
 
-    cols = pl.ds(0, SIDE)
-    x_halo = halo_copies(
-        x_hbm.at[0, :, cols, :], xhalo.at[1], x_hbm.at[rows - 1, :, cols, :], xhalo.at[0], 0
-    )
+    last_row = pl.ds((rows - 1) * PITCH, PITCH)
+    x_halo = halo_copies(x_hbm.at[pl.ds(0, PITCH)], xhalo.at[1], x_hbm.at[last_row], xhalo.at[0], 0)
     halo_start(x_halo)
 
     @pl.when(chan == 0)
@@ -241,62 +224,52 @@
         xhalo[1] = jnp.zeros(xhalo.shape[1:], BF16)
 
     def gather_buffer(p):
-        return pb if p == 0 else wb.at[p - 1]
+        return pb if isinstance(p, int) and p == 0 else wb.at[p - 1]
 
     def gather_z(p):
-        buffer = gather_buffer(p)
-        block = buffer.at[core, xc, yc, zc]
-        return [send(block, block, ag_s.at[p, k], ag_r.at[p, k], z_peer(k)) for k in (1, 2, 3)]
+        block = gather_buffer(p).at[core, xc, yc, zc]
+        return [remote(block, block, ag_s.at[p, k], ag_r.at[p, k], z_peer[k]) for k in (1, 2, 3)]
 
     def gather_xy(p):
         block = gather_buffer(p).at[core, xc, yc]
-        return [send(block, block, ag_s.at[p, 3 + k], ag_r.at[p, 3 + k], xy_peer(k)) for k in (1, 2, 3)]
+        return [remote(block, block, ag_s.at[p, 3 + k], ag_r.at[p, 3 + k], xy_peer[k]) for k in (1, 2, 3)]
 
     def gather_core(p):
         block = gather_buffer(p).at[core]
-        return [send(block, block, ag_s.at[p, 7], ag_r.at[p, 7], core_peer)]
-
-    def landed(copies):
-        for copy in copies:
-            copy.wait_recv()
+        return [remote(block, block, ag_s.at[p, 7], ag_r.at[p, 7], core_peer)]
 
     top = mask_ref[0:8, :].astype(F32).T
     for t in range(BANDS):
-        col_mask[t] = jnp.broadcast_to(top[0:SIDE, t : t + 1], (SIDE, 128))
-    step_in = lax.broadcasted_iota(jnp.int32, (SIDE, 128), 0)
-    not_first = (step_in > 0).astype(F32)
-    not_last = (step_in < SIDE - 1).astype(F32)
+        col_mask[t] = jnp.broadcast_to(top[:, t : t + 1], (BAND, 128))
 
     def two(block):
         return jnp.concatenate([block, block], axis=1)
 
-    def shift_row(block_of, row_flags, at, keep):
-        for t in range(BANDS):
-            valid = col_mask[t] * row_flags[t : t + 1, 0:1]
-            base = aligned(at + t * SIDE, 16)
-            act = jnp.maximum(block_of(t).astype(F32), 0.0) * two(valid)
-            shifted[pl.ds(base, SIDE), 256:512] = act.astype(BF16)
-            before = pltpu.roll(act, 1, 0) * two(not_first)
-            shifted[pl.ds(base, SIDE), 0:256] = before.astype(BF16)
-            after = pltpu.roll(act, SIDE - 1, 0) * two(not_last)
-            shifted[pl.ds(base, SIDE), 512:768] = after.astype(BF16)
-            if keep is not None:
-                mask_rows[pl.ds(aligned(keep + t * SIDE, 16), SIDE), :] = valid.astype(BF16)
-
-    def shift_chunk(k, carry):
-        flags = mask_ref[pl.ds(aligned((chan * rows + k * CHUNK_ROWS) * BANDS, 8), 8), :].astype(F32)
-        for r in range(CHUNK_ROWS):
-            row = k * CHUNK_ROWS + r
-            shift_row(
-                lambda t: xv[row, t],
-                flags[r * BANDS : (r + 1) * BANDS],
-                (row + 1) * PITCH,
-                row * PITCH,
-            )
+    def tile_mask(flags, n):
+        return col_mask[n % BANDS] * flags[n : n + 1, 0:1]
+
+    def row_flags(first_row, row_count):
+        first = aligned(first_row * BANDS, 8)
+        return mask_ref[pl.ds(first, row_count * BANDS), :].astype(F32)
+
+    def shift_tile(block, valid, at):
+        base = aligned(at, 16)
+        act = jnp.maximum(block.astype(F32), 0.0) * two(valid)
+        shifted[pl.ds(base, BAND), 256:512] = act.astype(BF16)
+        before = pltpu.roll(act, 1, 0)
+        shifted[pl.ds(base, BAND), 0:256] = before.astype(BF16)
+        after = pltpu.roll(act, BAND - 1, 0)
+        shifted[pl.ds(base, BAND), 512:768] = after.astype(BF16)
+
+    def shift_rows(k, carry):
+        flags = row_flags(chan * rows + k * 4, 4)
+        for n in range(4 * BANDS):
+            at = k * 4 * PITCH + n * BAND
+            shift_tile(xv[pl.ds(aligned(at, 16), BAND), :], tile_mask(flags, n), at + PITCH)
         return carry
 
     x_copy(0).wait()
-    shift_chunk(0, 0)
+    lax.fori_loop(0, 2, shift_rows, 0)
     pre.wait_recv()
     joined = wsend[core] + wpre[...]
     for i in range(3):
@@ -310,43 +283,40 @@
         axis=0,
     )
     pb[core, xc, yc, zc, 1] = quant.astype(BF16)
-    on_z = [gather_z(p) for p in range(4)]
+    for p in range(4):
+        start(gather_z(p))
 
     for k in range(1, chunks):
         x_copy(k).wait()
-    lax.fori_loop(1, chunks, shift_chunk, 0)
-    landed(on_z[0])
-    on_xy = [gather_xy(0)]
+    lax.fori_loop(2, rows // 4, shift_rows, 0)
+    landed(gather_z(0))
+    start(gather_xy(0))
     halo_wait_recv(x_halo)
 
     def halo_row(side, at, global_row, present):
-        first = aligned(lax.div(jnp.maximum(global_row, 0), 4) * 8, 8)
-        group = mask_ref[pl.ds(first, 8), :].astype(F32)
+        group = row_flags(lax.div(jnp.maximum(global_row, 0), 4) * 4, 4)
         inside = 2 * (3 if side == 0 else 0)
-        flags = group[inside : inside + 2]
-        scale = present.astype(F32)
-
-        shift_row(lambda t: xhalo[side, t], flags * scale, at, None)
+        flags = group[inside : inside + 2] * present.astype(F32)
+        for t in range(BANDS):
+            shift_tile(xhalo[side, t * BAND : (t + 1) * BAND], tile_mask(flags, t), at + t * BAND)
 
     halo_row(0, 0, chan * rows - 1, chan > 0)
     halo_row(1, (rows + 1) * PITCH, jnp.minimum(chan * rows + rows, 3 * rows), chan < 3)
 
-    landed(on_z[1])
-    on_xy.append(gather_xy(1))
-    landed(on_z[2])
-    on_xy.append(gather_xy(2))
-    landed(on_z[3])
-    on_xy.append(gather_xy(3))
-
-    dec_acc[...] = jnp.zeros_like(dec_acc)
-    proj_acc[...] = jnp.zeros_like(proj_acc)
+    landed(gather_z(1))
+    start(gather_xy(1))
+    landed(gather_z(2))
+    start(gather_xy(2))
+    landed(gather_z(3))
+    start(gather_xy(3))
+
     point_acc[...] = jnp.zeros_like(point_acc)
     book_acc[...] = jnp.zeros_like(book_acc)
     loss_acc[...] = jnp.zeros_like(loss_acc)
 
-    landed(on_xy[0])
-    on_core = [gather_core(0)]
-    landed(on_core[0])
+    landed(gather_xy(0))
+    start(gather_core(0))
+    landed(gather_core(0))
 
     blocks = [(h, x, y, z) for z in range(4) for y in range(2) for x in range(2) for h in range(2)]
     for h, x, y, z in blocks:
@@ -368,40 +338,39 @@
         entries = lax.broadcasted_iota(jnp.int32, (book_t.shape[1], CHUNK), 0)
         return (entries == ids_ref[k]).astype(F32).astype(BF16)
 
-    def chunk_of(ref, k):
-        return ref[pl.ds(aligned(k * CHUNK, 16), CHUNK), :]
-
-    def pixels_of(ref, k):
-        return ref[pl.ds(k * CHUNK_ROWS, CHUNK_ROWS)].reshape(CHUNK, 256)
-
-    def decoder_chunk(k, carry):
-        valid = chunk_of(mask_rows, k).astype(F32)
-        kept = (pixels_of(cotv, k).astype(F32) * two(valid)).astype(BF16)
+    def rows_of(k):
+        return pl.ds(aligned(k * CHUNK, CHUNK), CHUNK)
+
+    def valid_of(k):
+        flags = row_flags(chan * rows + k * CHUNK_ROWS, CHUNK_ROWS)
+        return jnp.concatenate([tile_mask(flags, n) for n in range(CHUNK_ROWS * BANDS)], axis=0)
+
+    def decoder_chunk(k):
+        kept = (cotv[rows_of(k), :].astype(F32) * two(valid_of(k))).astype(BF16)
+        cotv[rows_of(k), :] = kept
         chosen = dot(book_t[...], onehot_t(k)).T
         both = chosen + dot(kept, decz[...])
-        u_rows[pl.ds(aligned(k * CHUNK, 16), CHUNK), :] = both
-        both_low = both.astype(BF16)
-        ub_rows[pl.ds(aligned(k * CHUNK, 16), CHUNK), :] = both_low
-        dec_acc[...] += dot_rows(kept, both_low)
+        u_rows[rows_of(k), :] = both
+        lg_rows[rows_of(k), :] = both.astype(BF16)
+
+    def decoder_step(k, carry):
+        cot_copy(k).wait()
+        decoder_chunk(k)
+
+        @pl.when(k < 3)
+        def _():
+            landed(gather_xy(k + 1))
+            start(gather_core(k + 1))
+
         return carry
 
-    for k in range(chunks):
-        cot_copy(k).wait()
-    lax.fori_loop(0, 2, decoder_chunk, 0)
-    landed(on_xy[1])
-    on_core.append(gather_core(1))
-    lax.fori_loop(2, 4, decoder_chunk, 0)
-    landed(on_xy[2])
-    on_core.append(gather_core(2))
-    lax.fori_loop(4, 6, decoder_chunk, 0)
-    landed(on_xy[3])
-    on_core.append(gather_core(3))
-    lax.fori_loop(6, chunks, decoder_chunk, 0)
-    ub_copy = pltpu.make_async_copy(ub_rows, ub_hbm, ub_sem)
+    lax.fori_loop(0, chunks, decoder_step, 0)
+    ub_copy = pltpu.make_async_copy(lg_rows, ub_hbm, ub_sem)
     ub_copy.start()
+    dec_acc[...] = dot_rows(lg_rows[...], cotv[...]).T
 
     for i in range(3):
-        landed(on_core[1 + i])
+        landed(gather_core(1 + i))
         for h, x, y, z in blocks:
             for j in range(3):
                 first = j * 256 + z * 64 + y * 32 + h * 16
@@ -409,36 +378,44 @@
         for j in range(3):
             wback[i, :, j * 256 : j * 256 + 256] = wfull[i, j * 256 : j * 256 + 256, :].T
 
-    def forward_chunk(k, carry):
+    def middle_chunk(k, carry):
         hidden = None
         for i in range(3):
-            window = shifted[pl.ds(aligned((k * CHUNK_ROWS + i) * PITCH, 16), CHUNK), :]
+            window = shifted[pl.ds(aligned((k * CHUNK_ROWS + i) * PITCH, PITCH), CHUNK), :]
             term = dot(window, wfull[i])
             hidden = term if hidden is None else hidden + term
-        middle = jnp.maximum(hidden, 0.0).astype(BF16)
+        cotv[rows_of(k), :] = jnp.maximum(hidden, 0.0).astype(BF16)
+        return carry
+
+    def latent_chunk(k, carry):
+        middle = cotv[rows_of(k), :]
         branch = dot(middle, point_n[...])
-        summed = (pixels_of(xv, k).astype(F32) + branch).astype(BF16)
-        valid = chunk_of(mask_rows, k).astype(F32)
-        gap = chunk_of(u_rows, k) - dot(summed, projz[...])
+        summed = (xv[rows_of(k), :].astype(F32) + branch).astype(BF16)
+        xv[rows_of(k), :] = summed
+        valid = valid_of(k)
+        gap = u_rows[rows_of(k), :] - dot(summed, projz[...])
         weighted = gap * valid
         loss_acc[...] += jnp.sum((weighted * gap).reshape(CHUNK // 8, 8, 128), axis=0)
         latent_grad = (gap - 0.5 * pltpu.roll(weighted, LAT, 1)).astype(BF16)
-        lg_rows[pl.ds(aligned(k * CHUNK, 16), CHUNK), :] = latent_grad
+        lg_rows[rows_of(k), :] = latent_grad
         term = 2.0 * weighted
         coarse = term.astype(BF16).astype(F32)
-        fine = pltpu.roll(term - coarse, LAT, 1)
-        parts = jnp.where(high, coarse, fine).astype(BF16)
-        book_acc[...] += dot(onehot_t(k), parts)
-        proj_acc[...] += dot_rows(summed, latent_grad)
+        u_rows[rows_of(k), :] = jnp.where(high, coarse, pltpu.roll(term - coarse, LAT, 1))
         resid_low = dot(latent_grad, proj_t[...]).astype(BF16)
         point_acc[...] += dot_rows(resid_low, middle)
         back = dot(resid_low, point_t[...])
-        hidden_grad = jnp.where(hidden > 0.0, back, 0.0).astype(BF16)
-        hgp[pl.ds(aligned((k * CHUNK_ROWS + 1) * PITCH, 16), CHUNK), :] = hidden_grad
-        hgt[:, pl.ds(aligned(k * CHUNK, 128), CHUNK)] = hidden_grad.T
+        hidden_grad = jnp.where(middle.astype(F32) > 0.0, back, 0.0).astype(BF16)
+        hgp[pl.ds(aligned((k * CHUNK_ROWS + 1) * PITCH, PITCH), CHUNK), :] = hidden_grad
+        hgt[:, pl.ds(aligned(k * CHUNK, CHUNK), CHUNK)] = hidden_grad.T
         return carry
 
-    lax.fori_loop(0, chunks, forward_chunk, 0)
+    def book_chunk(k, carry):
+        book_acc[...] += dot(onehot_t(k), u_rows[rows_of(k), :].astype(BF16))
+        return carry
+
+    lax.fori_loop(0, chunks, middle_chunk, 0)
+    ub_copy.wait()
+    lax.fori_loop(0, chunks, latent_chunk, 0)
 
     zero_row = jnp.zeros((PITCH, 256), BF16)
 
@@ -457,37 +434,44 @@
     halo_start(hg_halo)
 
     def reduce_buffers(p):
-        if p == 0:
+        if isinstance(p, int) and p == 0:
             return gp, rp0, rp1, rp2
         return gs.at[p - 1], rc0.at[p - 1], rc1.at[p - 1], rc2.at[p - 1]
 
     def reduce_core(p):
         buffer, first, _, _ = reduce_buffers(p)
-        return [send(buffer.at[1 - core], first, rs_s.at[p, 0], rs_r.at[p, 0], core_peer)]
-
-    def reduce_xy(p, copies):
-        landed(copies)
-        buffer, first, second, _ = reduce_buffers(p)
-        buffer[core] = buffer[core] + first[...]
-        out = []
-        for k in (1, 2, 3):
-            x_new, y_new = xy_of(k)
-            out.append(
-                send(buffer.at[core, x_new, y_new], second.at[k - 1], rs_s.at[p, k], rs_r.at[p, k], xy_peer(k))
-            )
-        return out
-
-    def reduce_z(p, copies):
-        landed(copies)
-        buffer, _, second, third = reduce_buffers(p)
-        buffer[core, xc, yc] = (buffer[core, xc, yc] + second[0]) + (second[1] + second[2])
+        return [remote(buffer.at[other_core], first, rs_s.at[p, 0], rs_r.at[p, 0], core_peer)]
+
+    def reduce_xy(p):
+        buffer, _, second, _ = reduce_buffers(p)
         return [
-            send(buffer.at[core, xc, yc, z_of(k)], third.at[k - 1], rs_s.at[p, 3 + k], rs_r.at[p, 3 + k], z_peer(k))
+            remote(buffer.at[core, *xy_of[k]], second.at[k - 1], rs_s.at[p, k], rs_r.at[p, k], xy_peer[k])
             for k in (1, 2, 3)
         ]
 
-    def reduce_end(p, copies):
-        landed(copies)
+    def reduce_z(p):
+        buffer, _, _, third = reduce_buffers(p)
+        return [
+            remote(
+                buffer.at[core, xc, yc, z_of[k]], third.at[k - 1], rs_s.at[p, 3 + k], rs_r.at[p, 3 + k], z_peer[k]
+            )
+            for k in (1, 2, 3)
+        ]
+
+    def core_to_xy(p):
+        landed(reduce_core(p))
+        buffer, first, _, _ = reduce_buffers(p)
+        buffer[core] = buffer[core] + first[...]
+        start(reduce_xy(p))
+
+    def xy_to_z(p):
+        landed(reduce_xy(p))
+        buffer, _, second, _ = reduce_buffers(p)
+        buffer[core, xc, yc] = (buffer[core, xc, yc] + second[0]) + (second[1] + second[2])
+        start(reduce_z(p))
+
+    def reduce_end(p):
+        landed(reduce_z(p))
         buffer, _, _, third = reduce_buffers(p)
         total = (buffer[core, xc, yc, zc] + third[0]) + (third[1] + third[2])
         if p == 0:
@@ -497,83 +481,105 @@
             for j in range(3):
                 fin[3 * (p - 1) + j] = total[j * 16 : j * 16 + 16]
 
-    counts = mask_ref[pl.ds(aligned(chan * rows * BANDS, 8), rows * BANDS), :].astype(F32)
-    counts = jnp.sum(counts.reshape(rows * BANDS // 8, 8, 128), axis=0)
-    tallies = jnp.where(high, loss_acc[...], counts + pltpu.roll(counts, LAT, 1))
-    heads = jnp.where(high, dec_acc[...], proj_acc[...])
-    book_sum = book_acc[...] + pltpu.roll(book_acc[...], LAT, 1)
-    for h, x, y, z in blocks:
-        first = z * 64 + y * 32 + h * 16
-        owner = (2 * z + y) * 4 + 2 * x + h
-        gp[h, x, y, z, 0:16] = point_acc[first : first + 16, x * 128 : x * 128 + 128]
-        gp[h, x, y, z, 16:24] = heads[owner * 8 : owner * 8 + 8]
-        gp[h, x, y, z, 24:32] = jnp.where(
-            high, book_sum[owner * 16 + 8 : owner * 16 + 16], book_sum[owner * 16 : owner * 16 + 8]
-        )
-        gp[h, x, y, z, 32:40] = tallies
-    stage = [reduce_core(0), None, None, None]
-
     def conv_grad(i):
-        product = dot(hgt[...], shifted[i * PITCH : i * PITCH + pixels, :])
+        window = shifted[pl.ds(aligned(i * PITCH, PITCH), pixels), :]
+        product = dot(hgt[...], window)
         for j in range(3):
             turned = product[:, j * 256 : j * 256 + 256].T
             for h, x, y, z in blocks:
                 first = z * 64 + y * 32 + h * 16
                 gs[i, h, x, y, z, j * 16 : j * 16 + 16] = turned[first : first + 16, x * 128 : x * 128 + 128]
 
-    conv_grad(0)
-    stage[1] = reduce_core(1)
-    stage[0] = reduce_xy(0, stage[0])
-    conv_grad(1)
-    stage[2] = reduce_core(2)
-    stage[1] = reduce_xy(1, stage[1])
-    conv_grad(2)
-    stage[3] = reduce_core(3)
-    stage[2] = reduce_xy(2, stage[2])
-    stage[0] = reduce_z(0, stage[0])
+    def pack_small():
+        counts = mask_ref[pl.ds(aligned(chan * rows * BANDS, 8), rows * BANDS), :].astype(F32)
+        counts = jnp.sum(counts.reshape(rows * BANDS // 8, 8, 128), axis=0)
+        tallies = jnp.where(high, loss_acc[...], counts + pltpu.roll(counts, LAT, 1))
+        heads = jnp.where(high, dec_acc[...], proj_acc[...])
+        book_sum = book_acc[...] + pltpu.roll(book_acc[...], LAT, 1)
+        for h, x, y, z in blocks:
+            first = z * 64 + y * 32 + h * 16
+            owner = (2 * z + y) * 4 + 2 * x + h
+            gp[h, x, y, z, 0:16] = point_acc[first : first + 16, x * 128 : x * 128 + 128]
+            gp[h, x, y, z, 16:24] = heads[owner * 8 : owner * 8 + 8]
+            gp[h, x, y, z, 24:32] = jnp.where(
+                high, book_sum[owner * 16 + 8 : owner * 16 + 16], book_sum[owner * 16 : owner * 16 + 8]
+            )
+            gp[h, x, y, z, 32:40] = tallies
+
+    def grad_step(i, carry):
+        conv_grad(i)
+        start(reduce_core(i + 1))
+
+        @pl.when(i == 0)
+        def _():
+            lax.fori_loop(0, chunks, book_chunk, 0)
+            core_to_xy(1)
+
+        @pl.when(i == 1)
+        def _():
+            proj_acc[...] = proj_sum()
+            pack_small()
+            start(reduce_core(0))
+            core_to_xy(2)
+
+        @pl.when(i == 2)
+        def _():
+            core_to_xy(0)
+            xy_to_z(1)
+
+        return carry
+
+    def proj_sum():
+        return dot_rows(lg_rows[...], xv[...]).T
+
+    lax.fori_loop(0, 3, grad_step, 0)
     halo_wait_recv(hg_halo)
 
-    edge_first = two(not_first)[None]
-    edge_last = two(not_last)[None]
-
     def out_copy(k):
-        part = pl.ds(k * CHUNK_ROWS, CHUNK_ROWS)
-        return pltpu.make_async_copy(cotv.at[part], ig_hbm.at[part], out_sem.at[k])
-
-    def back_chunk(k, carry):
-        total = None
-        for i in range(3):
-            window = hgp[pl.ds(aligned((k * CHUNK_ROWS + 2 - i) * PITCH, 16), CHUNK), :]
-            term = dot(window, wback[i])
-            total = term if total is None else total + term
-        segments = CHUNK // SIDE
-        before = pltpu.roll(total[:, 512:768], 1, 0).reshape(segments, SIDE, 256) * edge_first
-        after = pltpu.roll(total[:, 0:256], CHUNK - 1, 0).reshape(segments, SIDE, 256) * edge_last
-        back_grad = total[:, 256:512] + (before + after).reshape(CHUNK, 256)
-        slope = shifted[pl.ds(aligned((k * CHUNK_ROWS + 1) * PITCH, 16), CHUNK), 256:512].astype(F32) > 0.0
-        resid = dot(chunk_of(lg_rows, k), proj_t[...])
-        grad = (resid + jnp.where(slope, back_grad, 0.0)).astype(BF16)
-        cotv[pl.ds(k * CHUNK_ROWS, CHUNK_ROWS)] = grad.reshape(CHUNK_ROWS, BANDS, SIDE, 256)
+        return pltpu.make_async_copy(cotv.at[part(k)], ig_hbm.at[part(k)], out_sem.at[k])
+
+    def back_chunk(k):
+        back_grad = None
+        for j in (1, 0, 2):
+            total = None
+            for i in range(3):
+                window = hgp[pl.ds(aligned((k * CHUNK_ROWS + 2 - i) * PITCH, PITCH), CHUNK), :]
+                term = dot(window, wback[i, :, j * 256 : j * 256 + 256])
+                total = term if total is None else total + term
+            if j != 1:
+                total = pltpu.roll(total, CHUNK - 1 if j == 0 else 1, 0)
+            back_grad = total if back_grad is None else back_grad + total
+        centre = pl.ds(aligned((k * CHUNK_ROWS + 1) * PITCH, PITCH), CHUNK)
+        slope = shifted[centre, 256:512].astype(F32) > 0.0
+        resid = dot(lg_rows[rows_of(k), :], proj_t[...])
+        cotv[rows_of(k), :] = (resid + jnp.where(slope, back_grad, 0.0)).astype(BF16)
+
+    def back_step(k, carry):
+        back_chunk(k)
+        out_copy(k).start()
+
+        @pl.when(k == 0)
+        def _():
+            core_to_xy(3)
+            xy_to_z(2)
+            reduce_end(1)
+
+        @pl.when(k == 1)
+        def _():
+            xy_to_z(0)
+
+        @pl.when(k == 2)
+        def _():
+            reduce_end(2)
+            xy_to_z(3)
+
         return carry
 
-    def back_chunks(first, last):
-        lax.fori_loop(first, last, back_chunk, 0)
-        for k in range(first, last):
-            out_copy(k).start()
-
-    back_chunks(0, 1)
-    stage[3] = reduce_xy(3, stage[3])
-    back_chunks(1, 3)
-    stage[1] = reduce_z(1, stage[1])
-    reduce_end(0, stage[0])
-    back_chunks(3, 5)
-    stage[2] = reduce_z(2, stage[2])
-    reduce_end(1, stage[1])
-    back_chunks(5, chunks)
-    stage[3] = reduce_z(3, stage[3])
-    reduce_end(2, stage[2])
-    reduce_end(3, stage[3])
-    last = send(fin, rx3, rs_s.at[0, 7], rs_r.at[0, 7], core_peer)
+    lax.fori_loop(0, chunks, back_step, 0)
+    reduce_end(0)
+    reduce_end(3)
+    last = remote(fin, rx3, rs_s.at[0, 7], rs_r.at[0, 7], core_peer)
+    last.start()
     last.wait_recv()
     mine, other = fin[...], rx3[...]
     is_first = core == 0
@@ -584,11 +590,12 @@
 
     for k in range(chunks):
         out_copy(k).wait()
-    ub_copy.wait()
     halo_wait_send(x_halo)
     halo_wait_send(hg_halo)
-    for copy in pending:
-        copy.wait_send()
+    sent([pre, last])
+    for p in range(4):
+        sent(gather_z(p) + gather_xy(p) + gather_core(p))
+        sent(reduce_core(p) + reduce_xy(p) + reduce_z(p))
 
 
 def finish_kernel(
@@ -598,21 +605,20 @@
     out_ref, grad_ref, loss_ref, *updates,
 ):
     step = pl.program_id(0)
-    steps_rows = out_ref.shape[0]
+    tiles = out_ref.shape[0] // BAND
     chan = lax.axis_index("chan")
-    first = (chan * pl.num_programs(0) + step) * steps_rows * BANDS
-    flags = mask_ref[pl.ds(aligned(first, 8), steps_rows * BANDS), :].astype(F32)
+    first = (chan * pl.num_programs(0) + step) * tiles
+    flags = mask_ref[pl.ds(aligned(first, 8), tiles), :].astype(F32)
     top = mask_ref[0:8, :].astype(F32).T
+    columns = [jnp.broadcast_to(top[:, t : t + 1], (BAND, 256)) for t in range(BANDS)]
     decoded = lax.dot_general(
         ub_ref[...], dec_ref[...], (((1,), (1,)), ((), ())), preferred_element_type=F32
     )
-    decoded = decoded.reshape(steps_rows, BANDS, SIDE, 256)
-    for r in range(steps_rows):
-        for t in range(BANDS):
-            at = r * BANDS + t
-            valid = top[0:SIDE, t : t + 1] * flags[at : at + 1, 0:1]
-            out_ref[r, t, 0:SIDE, :] = (decoded[r, t] * valid).astype(BF16)
-            grad_ref[r, t, 0:SIDE, :] = ig_ref[r, t]
+    for n in range(tiles):
+        part = slice(n * BAND, (n + 1) * BAND)
+        valid = columns[n % BANDS] * flags[n : n + 1, 0:1]
+        out_ref[part, :] = (decoded[part] * valid).astype(BF16)
+    grad_ref[...] = ig_ref[...]
 
     @pl.when(step == 0)
     def _():
@@ -622,11 +628,11 @@
         gap = jnp.sum(jnp.where(high, q[16:24], 0.0))
         count = jnp.sum(jnp.where(high, 0.0, q[16:24]))
         ratio = jnp.full((8, 128), gap, F32) / jnp.full((8, 128), count * LAT, F32)
-        row = lax.broadcasted_iota(jnp.int32, (8, 128), 0)
-        loss_ref[...] = jnp.where(row == 0, ratio, 0.25 * ratio)
+        loss_ref[0] = ratio[0, 0]
+        loss_ref[1] = 0.25 * ratio[0, 0]
         sets = (
             (g_ref[0:9], conv_w, conv_m, conv_v, 0.01),
-            (g_ref[9].T, point_w, point_m, point_v, 0.03),
+            (g_ref[9], point_w, point_m, point_v, 0.03),
             (heads[:, 0:LAT], proj_w, proj_m, proj_v, 0.03),
             (jnp.concatenate([book[:, 0:LAT], book[:, LAT:]], axis=0), code_w, code_m, code_v, 0.5),
             (heads[:, LAT:], dec_w, dec_m, dec_v, 0.06),
@@ -652,21 +658,20 @@
     dec_weight, dec_first, dec_second,
 ):
     channels = inputs.shape[1]
-    rows = inputs.shape[0] // (BANDS * BAND)
+    rows = inputs.shape[0] // PITCH
     chunks = rows // CHUNK_ROWS
     pixels = rows * PITCH
     padded = pixels + 2 * PITCH
     entries = 32 * code_book.shape[0]
-    canvas = (rows, BANDS, BAND, channels)
     mask = valid_mask.reshape(-1, BAND)
-    ids = code_ids.reshape(rows * BANDS, BAND)[:, :SIDE].reshape(chunks, 1, CHUNK)
-    packed = (rows, BANDS, SIDE, channels)
+    ids = code_ids.reshape(chunks, 1, CHUNK)
+    point_weight, point_first, point_second = point_weight.T, point_first.T, point_second.T
     dma = pltpu.SemaphoreType.DMA
     ub, ig, grads, quant, decoder = pl.pallas_call(
         functools.partial(block_kernel, rows),
         out_shape=(
             jax.ShapeDtypeStruct((pixels, 128), BF16),
-            jax.ShapeDtypeStruct(packed, BF16),
+            jax.ShapeDtypeStruct((pixels, channels), BF16),
             jax.ShapeDtypeStruct((10, 32, LAT), F32),
             jax.ShapeDtypeStruct((24, 128), F32),
             jax.ShapeDtypeStruct((channels, 128), BF16),
@@ -674,14 +679,12 @@
         in_specs=[anywhere()] * 2 + [vmem()] * 7,
         out_specs=(anywhere(), anywhere(), vmem(), vmem(), vmem()),
         scratch_shapes=[
-            pltpu.VMEM(packed, BF16),
-            pltpu.VMEM((2, BANDS, SIDE, channels), BF16),
-            pltpu.VMEM(packed, BF16),
+            pltpu.VMEM((pixels, channels), BF16),
+            pltpu.VMEM((2, PITCH, channels), BF16),
+            pltpu.VMEM((pixels, channels), BF16),
             pltpu.VMEM((padded, 3 * channels), BF16),
-            pltpu.VMEM((pixels, 128), BF16),
-            pltpu.VMEM((BANDS, SIDE, 128), F32),
+            pltpu.VMEM((BANDS, BAND, 128), F32),
             pltpu.VMEM((pixels, 128), F32),
-            pltpu.VMEM((pixels, 128), BF16),
             pltpu.VMEM((pixels, 128), BF16),
             pltpu.VMEM((padded, channels), BF16),
             pltpu.VMEM((channels, pixels), BF16),
@@ -726,11 +729,11 @@
             dma((4, 8)),
         ],
         compiler_params=pltpu.CompilerParams(
-            collective_id=0, has_side_effects=True, vmem_limit_bytes=60 * 2**20
+            collective_id=0, has_side_effects=True, vmem_limit_bytes=62 * 2**20
         ),
         name="block",
     )(
-        inputs.reshape(canvas), cotangent.reshape(canvas), ids, mask,
+        inputs, cotangent, ids, mask,
         conv_weight, point_weight, proj_weight, code_book, dec_weight,
     )
 
@@ -739,7 +742,7 @@
         proj_weight, proj_first, proj_second, code_book, code_first, code_second,
         dec_weight, dec_first, dec_second,
     )
-    tiles = pl.BlockSpec((CHUNK_ROWS, BANDS, BAND, channels), lambda n: (n, 0, 0, 0))
+    tiles = pl.BlockSpec((CHUNK, channels), lambda n: (n, 0))
 
     def whole(shape):
         return pl.BlockSpec(shape, lambda n: (0,) * len(shape))
@@ -754,13 +757,13 @@
         finish_kernel,
         grid=(chunks,),
         out_shape=(
-            jax.ShapeDtypeStruct(canvas, BF16),
-            jax.ShapeDtypeStruct(canvas, BF16),
-            jax.ShapeDtypeStruct((8, 128), F32),
+            jax.ShapeDtypeStruct(inputs.shape, BF16),
+            jax.ShapeDtypeStruct(inputs.shape, BF16),
+            jax.ShapeDtypeStruct((2,), F32),
             *updates,
         ),
         in_specs=[
-            pl.BlockSpec((CHUNK_ROWS, BANDS, SIDE, channels), lambda n: (n, 0, 0, 0)),
+            tiles,
             pl.BlockSpec((CHUNK, 128), lambda n: (n, 0)),
             whole(mask.shape),
             whole(decoder.shape),
@@ -768,17 +771,12 @@
             whole(quant.shape),
             *[whole(s.shape) for s in states],
         ],
-        out_specs=(tiles, tiles, whole((8, 128)), *specs),
-        compiler_params=pltpu.CompilerParams(vmem_limit_bytes=40 * 2**20),
+        out_specs=(tiles, tiles, pl.BlockSpec(memory_space=pltpu.SMEM), *specs),
+        compiler_params=pltpu.CompilerParams(vmem_limit_bytes=62 * 2**20),
         name="finish",
     )(ig, ub, mask, decoder, grads, quant, *states)
-    output, input_grad, ratio = results[:3]
-    return (
-        output.reshape(inputs.shape),
-        input_grad.reshape(inputs.shape),
-        ratio[0:2, 0],
-        *results[3:],
-    )
+    point_new = tuple(block.T for block in results[7:11])
+    return (*results[:7], *point_new, *results[11:])
 
 
 def row_stride():

time: 118 us -> 84.4 us (0.72)
  Pallas kernels: 104 us -> 83.3 us
  local copies, waits for them, and re-layouts: 12.7 us -> 0 us
    pallas_call x1, Pallas kernels: 97 us -> 75 us  [on_device(): pl.pallas_call(functools.partial(block_kernel, rows), out_shape=(jax.Shap...]
    unnamed x45 -> x0, local copies, waits for them, and re-layouts: 12 us -> none
    pallas_call x1, Pallas kernels: 6.71 us -> 8.27 us  [on_device(): pl.pallas_call(finish_kernel, grid=(chunks,), out_shape=(jax.ShapeDtypeSt...]
where the time goes in v2:
time: 84.4 us; the launch traced here: 84.1 us
  Pallas kernels  83.3 us (99%)
    pallas_call x1, Pallas kernels, on_device(): pl.pallas_call(functools.partial(block_kernel, rows), out_shape=(jax.Shap...  75 us
    pallas_call x1, Pallas kernels, on_device(): pl.pallas_call(finish_kernel, grid=(chunks,), out_shape=(jax.ShapeDtypeSt...  8.27 us

profile of v2, /device:TPU:0, one launch (start us, length us, event | category | flops | bytes accessed | tf_op | source)
XLA Modules:
  0.0 84.1 jit_solution(12030762041023252154)
XLA Ops:
  0.7 75.0 %block.1 = (bf16[8192,128]{1,0:T(8,128)(2,1)}, bf16[8192,256]{1,0:T(8,128)(2,1)}, f32[10,32,64]{2,1,0:T(8,128)}, f32[24,128]{1,0:T(8,128)}, bf16[256,128]{1,0:T(8,128)(2,1)}) custom-call(bf16[8192,256]{1,0:T(8,128)(2,1)} %x_hbm.1, bf16[8192,256]{1,0:T(8,128)(2,1)} %cot_hbm.1, s32[4,1,2048]{2,1,0:T(1,128)} %bitcast.13, s32[256,128]{1,0:T(8,128)} %bitcast.9, ...), custom_call_target="tpu_custom_call" | custom-call | tf_op jit(solution)/shard_map/block/pallas_call | solution.py:670
  75.7 8.3 %finish.1 = (bf16[8192,256]{1,0:T(8,128)(2,1)}, bf16[8192,256]{1,0:T(8,128)(2,1)}, f32[2]{0:T(128)}, f32[9,32,64]{2,1,0:T(8,128)}, f32[9,32,64]{2,1,0:T(8,128)},...) custom-call(bf16[8192,256]{1,0:T(8,128)(2,1)} %get-tuple-element.51., ...), custom_call_target="tpu_custom_call" | custom-call | tf_op jit(solution)/shard_map/finish/pallas_call | solution.py:756

commit v3 on v2

--- a/solution.py
+++ b/solution.py
@@ -14,6 +14,8 @@
 PITCH = BANDS * BAND
 CHUNK_ROWS = 8
 CHUNK = CHUNK_ROWS * PITCH
+BACK_ROWS = 4
+BACK = BACK_ROWS * PITCH
 MESH = pl.DeviceIdType.MESH
 F32 = jnp.float32
 BF16 = jnp.bfloat16
@@ -51,6 +53,18 @@
     rows,
     x_hbm,
     cot_hbm,
+    ids_hbm,
+    mask_hbm,
+    conv_hbm,
+    point_hbm,
+    proj_hbm,
+    book_hbm,
+    dec_hbm,
+    ub_hbm,
+    ig_hbm,
+    g_ref,
+    q_ref,
+    dz_ref,
     ids_ref,
     mask_ref,
     conv_ref,
@@ -58,11 +72,6 @@
     proj_ref,
     book_ref,
     dec_ref,
-    ub_hbm,
-    ig_hbm,
-    g_ref,
-    q_ref,
-    dz_ref,
     xv,
     xhalo,
     cotv,
@@ -72,10 +81,10 @@
     lg_rows,
     hgp,
     hgt,
-    wsend,
-    wpre,
     wb,
     pb,
+    qb,
+    hidden_rows,
     wfull,
     wback,
     point_t,
@@ -92,15 +101,18 @@
     book_acc,
     loss_acc,
     gp,
+    gb,
     gs,
     rp0,
     rp1,
     rp2,
+    rb0,
+    rb1,
+    rb2,
     rc0,
     rc1,
     rc2,
-    fin,
-    rx3,
+    small_sem,
     x_sem,
     cot_sem,
     out_sem,
@@ -141,43 +153,66 @@
         for copy in copies:
             copy.wait_send()
 
-    def part(k):
-        return pl.ds(k * CHUNK, CHUNK)
-
-    def x_copy(k):
-        return pltpu.make_async_copy(x_hbm.at[part(k)], xv.at[part(k)], x_sem.at[k])
-
-    def cot_copy(k):
-        return pltpu.make_async_copy(cot_hbm.at[part(k)], cotv.at[part(k)], cot_sem.at[k])
-
-    for k in range(chunks):
-        x_copy(k).start()
-    for k in range(chunks):
-        cot_copy(k).start()
-
-    lane = lax.broadcasted_iota(jnp.int32, (1, 128), 1)
-    high = lane >= LAT
-    own_half = high.astype(jnp.int32) == core
-
-    def wide(block):
-        return jnp.where(own_half, jnp.concatenate([block, block], axis=-1), 0.0).astype(BF16)
-
-    conv_wide = wide(conv_ref[...])
-    point_wide = wide(point_ref[...])
-    for half in range(2):
-        sixteen = slice(half * 16, half * 16 + 16)
-        wsend[half, 0:9] = conv_wide[:, sixteen]
-        wsend[half, 9] = point_wide[sixteen]
-
     barrier = pltpu.get_barrier_semaphore()
     partners = [core_peer, (dp, 3 - chan)]
     partners += xy_peer[1:] + z_peer[1:]
     for partner in partners:
         pl.semaphore_signal(barrier, inc=1, device_id=partner, device_id_type=MESH)
+
+    smalls = [
+        pltpu.make_async_copy(src, dst, small_sem.at[n])
+        for n, (src, dst) in enumerate(
+            (
+                (conv_hbm, conv_ref),
+                (point_hbm, point_ref),
+                (proj_hbm, proj_ref),
+                (book_hbm, book_ref),
+                (dec_hbm, dec_ref),
+                (mask_hbm, mask_ref),
+                (ids_hbm, ids_ref),
+            )
+        )
+    ]
+    for copy in smalls:
+        copy.start()
+
+    def part(k):
+        return pl.ds(k * CHUNK, CHUNK)
+
+    def x_copy(k):
+        return pltpu.make_async_copy(x_hbm.at[part(k)], xv.at[part(k)], x_sem.at[k])
+
+    def cot_copy(k):
+        return pltpu.make_async_copy(cot_hbm.at[part(k)], cotv.at[part(k)], cot_sem.at[k])
+
+    for k in range(chunks):
+        x_copy(k).start()
+    for k in range(chunks):
+        cot_copy(k).start()
+
+    lane = lax.broadcasted_iota(jnp.int32, (1, 128), 1)
+    high = lane >= LAT
+
+    def packed(block):
+        return jnp.concatenate([block[..., 0:16, :], block[..., 16:32, :]], axis=-1).astype(BF16)
+
+    for copy in smalls[0:5]:
+        copy.wait()
+    conv_own = packed(conv_ref[...])
+    for i in range(3):
+        wb[i, core, xc, yc, zc] = conv_own[3 * i : 3 * i + 3]
+    pb[core, xc, yc, zc] = packed(point_ref[...])
+    quant = jnp.concatenate(
+        [
+            jnp.concatenate([dec_ref[...], proj_ref[...]], axis=1),
+            jnp.concatenate([book_ref[0:8, :], book_ref[8:16, :]], axis=1),
+        ],
+        axis=0,
+    )
+    qb[core, xc, yc, zc] = quant.astype(BF16)
+
     pl.semaphore_wait(barrier, len(partners))
 
-    pre = remote(wsend.at[other_core], wpre, ag_s.at[0, 0], ag_r.at[0, 0], core_peer)
-    pre.start()
 
     def halo_copies(up_src, up_dst, down_src, down_dst, at):
         up = remote(up_src, up_dst, halo_s.at[at], halo_r.at[at], up_peer)
@@ -213,8 +248,6 @@
 
     last_row = pl.ds((rows - 1) * PITCH, PITCH)
     x_halo = halo_copies(x_hbm.at[pl.ds(0, PITCH)], xhalo.at[1], x_hbm.at[last_row], xhalo.at[0], 0)
-    halo_start(x_halo)
-
     @pl.when(chan == 0)
     def _():
         xhalo[0] = jnp.zeros(xhalo.shape[1:], BF16)
@@ -224,7 +257,9 @@
         xhalo[1] = jnp.zeros(xhalo.shape[1:], BF16)
 
     def gather_buffer(p):
-        return pb if isinstance(p, int) and p == 0 else wb.at[p - 1]
+        if isinstance(p, int) and p in (0, 4):
+            return qb if p == 0 else pb
+        return wb.at[p - 1]
 
     def gather_z(p):
         block = gather_buffer(p).at[core, xc, yc, zc]
@@ -237,6 +272,13 @@
     def gather_core(p):
         block = gather_buffer(p).at[core]
         return [remote(block, block, ag_s.at[p, 7], ag_r.at[p, 7], core_peer)]
+
+    for p in (0, 1, 2, 3, 4):
+        start(gather_z(p))
+    halo_start(x_halo)
+
+    for copy in smalls[5:]:
+        copy.wait()
 
     top = mask_ref[0:8, :].astype(F32).T
     for t in range(BANDS):
@@ -270,27 +312,14 @@
 
     x_copy(0).wait()
     lax.fori_loop(0, 2, shift_rows, 0)
-    pre.wait_recv()
-    joined = wsend[core] + wpre[...]
-    for i in range(3):
-        wb[i, core, xc, yc, zc] = joined[3 * i : 3 * i + 3]
-    pb[core, xc, yc, zc, 0] = joined[9]
-    quant = jnp.concatenate(
-        [
-            jnp.concatenate([dec_ref[...], proj_ref[...]], axis=1),
-            jnp.concatenate([book_ref[0:8, :], book_ref[8:16, :]], axis=1),
-        ],
-        axis=0,
-    )
-    pb[core, xc, yc, zc, 1] = quant.astype(BF16)
-    for p in range(4):
-        start(gather_z(p))
-
     for k in range(1, chunks):
         x_copy(k).wait()
-    lax.fori_loop(2, rows // 4, shift_rows, 0)
+    lax.fori_loop(2, 5, shift_rows, 0)
     landed(gather_z(0))
     start(gather_xy(0))
+    lax.fori_loop(5, rows // 4, shift_rows, 0)
+    landed(gather_z(1))
+    start(gather_xy(1))
     halo_wait_recv(x_halo)
 
     def halo_row(side, at, global_row, present):
@@ -303,30 +332,35 @@
     halo_row(0, 0, chan * rows - 1, chan > 0)
     halo_row(1, (rows + 1) * PITCH, jnp.minimum(chan * rows + rows, 3 * rows), chan < 3)
 
-    landed(gather_z(1))
-    start(gather_xy(1))
-    landed(gather_z(2))
-    start(gather_xy(2))
-    landed(gather_z(3))
-    start(gather_xy(3))
+    for p in (2, 3, 4):
+        landed(gather_z(p))
+        start(gather_xy(p))
+    landed(gather_xy(0))
+    start(gather_core(0))
 
     point_acc[...] = jnp.zeros_like(point_acc)
     book_acc[...] = jnp.zeros_like(book_acc)
     loss_acc[...] = jnp.zeros_like(loss_acc)
-
-    landed(gather_xy(0))
-    start(gather_core(0))
     landed(gather_core(0))
 
-    blocks = [(h, x, y, z) for z in range(4) for y in range(2) for x in range(2) for h in range(2)]
+    squares = [(x, y, z) for z in range(4) for y in range(2) for x in range(2)]
+    blocks = [(h, x, y, z) for x, y, z in squares for h in range(2)]
+
+    def natural(first, second):
+        lower = jnp.concatenate([first[:, 0:LAT], second[:, 0:LAT]], axis=1)
+        upper = jnp.concatenate([first[:, LAT:], second[:, LAT:]], axis=1)
+        return jnp.concatenate([lower, upper], axis=0)
+
+    def by_core(tile):
+        lower, upper = tile[0:16], tile[16:32]
+        return jnp.where(high, pltpu.roll(upper, LAT, 1), lower), jnp.where(high, upper, pltpu.roll(lower, LAT, 1))
+
     for h, x, y, z in blocks:
-        point_t[z * 64 + y * 32 + h * 16 : z * 64 + y * 32 + h * 16 + 16, x * 128 : x * 128 + 128] = pb[h, x, y, z, 0]
         owner = (2 * z + y) * 4 + 2 * x + h
-        small = pb[h, x, y, z, 1].astype(F32)
+        small = qb[h, x, y, z].astype(F32)
         qf[owner * 8 : owner * 8 + 8, :] = small[0:8]
         bookf[owner * 16 : owner * 16 + 8, :] = pltpu.roll(small[8:16], LAT, 1)
         bookf[owner * 16 + 8 : owner * 16 + 16, :] = small[8:16]
-    point_n[...] = point_t[...].T
     small = qf[...]
     decz[...] = jnp.where(high, 0.0, small).astype(BF16)
     projz[...] = jnp.where(high, small, 0.0).astype(BF16)
@@ -357,10 +391,10 @@
         cot_copy(k).wait()
         decoder_chunk(k)
 
-        @pl.when(k < 3)
+        @pl.when(k == 2)
         def _():
-            landed(gather_xy(k + 1))
-            start(gather_core(k + 1))
+            landed(gather_xy(1))
+            start(gather_core(1))
 
         return carry
 
@@ -369,21 +403,47 @@
     ub_copy.start()
     dec_acc[...] = dot_rows(lg_rows[...], cotv[...]).T
 
-    for i in range(3):
+    def unpack_taps(i):
         landed(gather_core(1 + i))
-        for h, x, y, z in blocks:
+        for x, y, z in squares:
             for j in range(3):
-                first = j * 256 + z * 64 + y * 32 + h * 16
-                wfull[i, first : first + 16, x * 128 : x * 128 + 128] = wb[i, h, x, y, z, j]
+                first = j * 256 + z * 64 + y * 32
+                wfull[i, first : first + 32, x * 128 : x * 128 + 128] = natural(wb[i, 0, x, y, z, j], wb[i, 1, x, y, z, j])
         for j in range(3):
             wback[i, :, j * 256 : j * 256 + 256] = wfull[i, j * 256 : j * 256 + 256, :].T
 
+    def taps(k, i):
+        window = shifted[pl.ds(aligned((k * CHUNK_ROWS + i) * PITCH, PITCH), CHUNK), :]
+        return dot(window, wfull[i])
+
+    def hidden_chunk(k, carry):
+        hidden_rows[rows_of(k), :] = taps(k, 0)
+
+        @pl.when(k == 0)
+        def _():
+            landed(gather_xy(2))
+            start(gather_core(2))
+
+        @pl.when(k == 1)
+        def _():
+            landed(gather_xy(3))
+            start(gather_core(3))
+
+        return carry
+
     def middle_chunk(k, carry):
-        hidden = None
-        for i in range(3):
-            window = shifted[pl.ds(aligned((k * CHUNK_ROWS + i) * PITCH, PITCH), CHUNK), :]
-            term = dot(window, wfull[i])
-            hidden = term if hidden is None else hidden + term
+        hidden = hidden_rows[rows_of(k), :] + (taps(k, 1) + taps(k, 2))
+        cotv[rows_of(k), :] = jnp.maximum(hidden, 0.0).astype(BF16)
+
+        @pl.when(k == 0)
+        def _():
+            landed(gather_xy(4))
+            start(gather_core(4))
+
+        return carry
+
+    def whole_chunk(k, carry):
+        hidden = taps(k, 0) + (taps(k, 1) + taps(k, 2))
         cotv[rows_of(k), :] = jnp.maximum(hidden, 0.0).astype(BF16)
         return carry
 
@@ -413,7 +473,17 @@
         book_acc[...] += dot(onehot_t(k), u_rows[rows_of(k), :].astype(BF16))
         return carry
 
-    lax.fori_loop(0, chunks, middle_chunk, 0)
+    unpack_taps(0)
+    lax.fori_loop(0, chunks // 2, hidden_chunk, 0)
+    unpack_taps(1)
+    unpack_taps(2)
+    lax.fori_loop(0, chunks // 2, middle_chunk, 0)
+    lax.fori_loop(chunks // 2, chunks, whole_chunk, 0)
+    landed(gather_core(4))
+    for x, y, z in squares:
+        first = z * 64 + y * 32
+        point_t[first : first + 32, x * 128 : x * 128 + 128] = natural(pb[0, x, y, z], pb[1, x, y, z])
+    point_n[...] = point_t[...].T
     ub_copy.wait()
     lax.fori_loop(0, chunks, latent_chunk, 0)
 
@@ -436,6 +506,8 @@
     def reduce_buffers(p):
         if isinstance(p, int) and p == 0:
             return gp, rp0, rp1, rp2
+        if isinstance(p, int) and p == 4:
+            return gb, rb0, rb1, rb2
         return gs.at[p - 1], rc0.at[p - 1], rc1.at[p - 1], rc2.at[p - 1]
 
     def reduce_core(p):
@@ -475,36 +547,46 @@
         buffer, _, _, third = reduce_buffers(p)
         total = (buffer[core, xc, yc, zc] + third[0]) + (third[1] + third[2])
         if p == 0:
-            q_ref[...] = total[16:40]
-            fin[9] = total[0:16]
+            q_ref[0:8] = total[16:24]
+            q_ref[16:24] = total[24:32]
+            g_ref[9] = total[0:16]
+        elif p == 4:
+            q_ref[8:16] = total
         else:
             for j in range(3):
-                fin[3 * (p - 1) + j] = total[j * 16 : j * 16 + 16]
+                g_ref[3 * (p - 1) + j] = total[j * 16 : j * 16 + 16]
 
     def conv_grad(i):
         window = shifted[pl.ds(aligned(i * PITCH, PITCH), pixels), :]
         product = dot(hgt[...], window)
         for j in range(3):
             turned = product[:, j * 256 : j * 256 + 256].T
-            for h, x, y, z in blocks:
-                first = z * 64 + y * 32 + h * 16
-                gs[i, h, x, y, z, j * 16 : j * 16 + 16] = turned[first : first + 16, x * 128 : x * 128 + 128]
+            for x, y, z in squares:
+                first = z * 64 + y * 32
+                halves = by_core(turned[first : first + 32, x * 128 : x * 128 + 128])
+                for h in range(2):
+                    gs[i, h, x, y, z, j * 16 : j * 16 + 16] = halves[h]
 
     def pack_small():
         counts = mask_ref[pl.ds(aligned(chan * rows * BANDS, 8), rows * BANDS), :].astype(F32)
         counts = jnp.sum(counts.reshape(rows * BANDS // 8, 8, 128), axis=0)
         tallies = jnp.where(high, loss_acc[...], counts + pltpu.roll(counts, LAT, 1))
         heads = jnp.where(high, dec_acc[...], proj_acc[...])
+        for x, y, z in squares:
+            first = z * 64 + y * 32
+            halves = by_core(point_acc[first : first + 32, x * 128 : x * 128 + 128])
+            for h in range(2):
+                gp[h, x, y, z, 0:16] = halves[h]
+        for h, x, y, z in blocks:
+            owner = (2 * z + y) * 4 + 2 * x + h
+            gp[h, x, y, z, 16:24] = heads[owner * 8 : owner * 8 + 8]
+            gp[h, x, y, z, 24:32] = tallies
+
+    def pack_book():
         book_sum = book_acc[...] + pltpu.roll(book_acc[...], LAT, 1)
         for h, x, y, z in blocks:
-            first = z * 64 + y * 32 + h * 16
-            owner = (2 * z + y) * 4 + 2 * x + h
-            gp[h, x, y, z, 0:16] = point_acc[first : first + 16, x * 128 : x * 128 + 128]
-            gp[h, x, y, z, 16:24] = heads[owner * 8 : owner * 8 + 8]
-            gp[h, x, y, z, 24:32] = jnp.where(
-                high, book_sum[owner * 16 + 8 : owner * 16 + 16], book_sum[owner * 16 : owner * 16 + 8]
-            )
-            gp[h, x, y, z, 32:40] = tallies
+            first = ((2 * z + y) * 4 + 2 * x + h) * 16
+            gb[h, x, y, z] = jnp.where(high, book_sum[first + 8 : first + 16], book_sum[first : first + 8])
 
     def grad_step(i, carry):
         conv_grad(i)
@@ -512,135 +594,168 @@
 
         @pl.when(i == 0)
         def _():
-            lax.fori_loop(0, chunks, book_chunk, 0)
-            core_to_xy(1)
-
-        @pl.when(i == 1)
+            core_to_xy(0)
+
+        @pl.when(i < 2)
         def _():
-            proj_acc[...] = proj_sum()
-            pack_small()
-            start(reduce_core(0))
-            core_to_xy(2)
-
-        @pl.when(i == 2)
-        def _():
-            core_to_xy(0)
-            xy_to_z(1)
+            lax.fori_loop(2 * i, 2 * i + 2, book_chunk, 0)
+            core_to_xy(i + 1)
 
         return carry
 
-    def proj_sum():
-        return dot_rows(lg_rows[...], xv[...]).T
-
+    proj_acc[...] = dot_rows(lg_rows[...], xv[...]).T
+    pack_small()
+    start(reduce_core(0))
     lax.fori_loop(0, 3, grad_step, 0)
+    pack_book()
+    start(reduce_core(4))
+    xy_to_z(0)
+    xy_to_z(1)
     halo_wait_recv(hg_halo)
 
+    def back_rows(k):
+        return pl.ds(aligned(k * BACK, BACK), BACK)
+
     def out_copy(k):
-        return pltpu.make_async_copy(cotv.at[part(k)], ig_hbm.at[part(k)], out_sem.at[k])
+        return pltpu.make_async_copy(cotv.at[back_rows(k)], ig_hbm.at[back_rows(k)], out_sem.at[k])
 
     def back_chunk(k):
         back_grad = None
         for j in (1, 0, 2):
             total = None
             for i in range(3):
-                window = hgp[pl.ds(aligned((k * CHUNK_ROWS + 2 - i) * PITCH, PITCH), CHUNK), :]
+                window = hgp[pl.ds(aligned((k * BACK_ROWS + 2 - i) * PITCH, PITCH), BACK), :]
                 term = dot(window, wback[i, :, j * 256 : j * 256 + 256])
                 total = term if total is None else total + term
             if j != 1:
-                total = pltpu.roll(total, CHUNK - 1 if j == 0 else 1, 0)
+                total = pltpu.roll(total, BACK - 1 if j == 0 else 1, 0)
             back_grad = total if back_grad is None else back_grad + total
-        centre = pl.ds(aligned((k * CHUNK_ROWS + 1) * PITCH, PITCH), CHUNK)
+        centre = pl.ds(aligned((k * BACK_ROWS + 1) * PITCH, PITCH), BACK)
         slope = shifted[centre, 256:512].astype(F32) > 0.0
-        resid = dot(lg_rows[rows_of(k), :], proj_t[...])
-        cotv[rows_of(k), :] = (resid + jnp.where(slope, back_grad, 0.0)).astype(BF16)
+        resid = dot(lg_rows[back_rows(k), :], proj_t[...])
+        grad = resid + jnp.where(slope, back_grad, 0.0)
+        cotv[back_rows(k), :] = grad.astype(BF16)
+
+    steps = {
+        0: [(core_to_xy, 3), (core_to_xy, 4)],
+        1: [(reduce_end, 0)],
+        2: [(xy_to_z, 2), (reduce_end, 1)],
+        5: [(xy_to_z, 3), (xy_to_z, 4)],
+        6: [(reduce_end, 2)],
+    }
 
     def back_step(k, carry):
         back_chunk(k)
         out_copy(k).start()
-
-        @pl.when(k == 0)
-        def _():
-            core_to_xy(3)
-            xy_to_z(2)
-            reduce_end(1)
-
-        @pl.when(k == 1)
-        def _():
-            xy_to_z(0)
-
-        @pl.when(k == 2)
-        def _():
-            reduce_end(2)
-            xy_to_z(3)
+        for at, todo in steps.items():
+
+            @pl.when(k == at)
+            def _():
+                for act, p in todo:
+                    act(p)
 
         return carry
 
-    lax.fori_loop(0, chunks, back_step, 0)
-    reduce_end(0)
+    lax.fori_loop(0, rows // BACK_ROWS, back_step, 0)
+    reduce_end(4)
     reduce_end(3)
-    last = remote(fin, rx3, rs_s.at[0, 7], rs_r.at[0, 7], core_peer)
-    last.start()
-    last.wait_recv()
-    mine, other = fin[...], rx3[...]
-    is_first = core == 0
-    lower = jnp.where(is_first, mine, other)
-    upper = jnp.where(is_first, other, mine)
-    whole = jnp.concatenate([lower, upper], axis=1)
-    g_ref[...] = jnp.where(is_first, whole[..., 0:LAT], whole[..., LAT:])
-
-    for k in range(chunks):
+
+    for k in range(rows // BACK_ROWS):
         out_copy(k).wait()
     halo_wait_send(x_halo)
     halo_wait_send(hg_halo)
-    sent([pre, last])
-    for p in range(4):
+    for p in range(5):
         sent(gather_z(p) + gather_xy(p) + gather_core(p))
         sent(reduce_core(p) + reduce_xy(p) + reduce_z(p))
 
 
-def finish_kernel(
-    ig_ref, ub_ref, mask_ref, dec_ref, g_ref, q_ref,
-    conv_w, conv_m, conv_v, point_w, point_m, point_v, proj_w, proj_m, proj_v,
-    code_w, code_m, code_v, dec_w, dec_m, dec_v,
-    out_ref, grad_ref, loss_ref, *updates,
-):
-    step = pl.program_id(0)
-    tiles = out_ref.shape[0] // BAND
+def finish_kernel(tile, ig_hbm, ub_hbm, *refs):
+    smalls, (out_hbm, grad_hbm, loss_ref), updates = refs[0:19], refs[19:22], refs[22:42]
+    ub_rows, out_rows, ig_rows = refs[42:45]
+    held, results = refs[45:64], refs[64:79]
+    ub_sem, out_sem, ig_sem, grad_sem, in_sem, end_sem = refs[79:]
+    tiles = ub_rows.shape[0] // tile
+
+    def part(k):
+        return pl.ds(k * tile, tile)
+
+    def ub_copy(k):
+        return pltpu.make_async_copy(ub_hbm.at[part(k)], ub_rows.at[part(k)], ub_sem.at[k])
+
+    def ig_copy(k):
+        return pltpu.make_async_copy(ig_hbm.at[part(k)], ig_rows.at[part(k)], ig_sem.at[k])
+
+    def grad_copy(k):
+        return pltpu.make_async_copy(ig_rows.at[part(k)], grad_hbm.at[part(k)], grad_sem.at[k])
+
+    def out_copy(k):
+        return pltpu.make_async_copy(out_rows.at[part(k)], out_hbm.at[part(k)], out_sem.at[k])
+
+    arrive = [pltpu.make_async_copy(src, dst, in_sem.at[n]) for n, (src, dst) in enumerate(zip(smalls, held))]
+    wide_updates = [ref for n, ref in enumerate(updates) if n % 4 < 3]
+    leave = [pltpu.make_async_copy(src, dst, end_sem.at[n]) for n, (src, dst) in enumerate(zip(results, wide_updates))]
+    for n in range(2):
+        arrive[n].start()
+    for k in range(tiles):
+        ub_copy(k).start()
+    for copy in arrive[2:]:
+        copy.start()
+    for k in range(tiles):
+        ig_copy(k).start()
+    mask_ref, dec_ref, g_ref, q_ref = held[0:4]
+    arrive[0].wait()
+    arrive[1].wait()
     chan = lax.axis_index("chan")
-    first = (chan * pl.num_programs(0) + step) * tiles
-    flags = mask_ref[pl.ds(aligned(first, 8), tiles), :].astype(F32)
     top = mask_ref[0:8, :].astype(F32).T
     columns = [jnp.broadcast_to(top[:, t : t + 1], (BAND, 256)) for t in range(BANDS)]
-    decoded = lax.dot_general(
-        ub_ref[...], dec_ref[...], (((1,), (1,)), ((), ())), preferred_element_type=F32
-    )
-    for n in range(tiles):
-        part = slice(n * BAND, (n + 1) * BAND)
-        valid = columns[n % BANDS] * flags[n : n + 1, 0:1]
-        out_ref[part, :] = (decoded[part] * valid).astype(BF16)
-    grad_ref[...] = ig_ref[...]
-
-    @pl.when(step == 0)
-    def _():
-        q = q_ref[...]
-        heads, book = q[0:8], q[8:16]
-        high = lax.broadcasted_iota(jnp.int32, (8, 128), 1) >= LAT
-        gap = jnp.sum(jnp.where(high, q[16:24], 0.0))
-        count = jnp.sum(jnp.where(high, 0.0, q[16:24]))
-        ratio = jnp.full((8, 128), gap, F32) / jnp.full((8, 128), count * LAT, F32)
-        loss_ref[0] = ratio[0, 0]
-        loss_ref[1] = 0.25 * ratio[0, 0]
-        sets = (
-            (g_ref[0:9], conv_w, conv_m, conv_v, 0.01),
-            (g_ref[9], point_w, point_m, point_v, 0.03),
-            (heads[:, 0:LAT], proj_w, proj_m, proj_v, 0.03),
-            (jnp.concatenate([book[:, 0:LAT], book[:, LAT:]], axis=0), code_w, code_m, code_v, 0.5),
-            (heads[:, LAT:], dec_w, dec_m, dec_v, 0.06),
+    inner = tile // BAND
+
+    def out_tile(k, carry):
+        ub_copy(k).wait()
+        here = pl.ds(aligned(k * tile, tile), tile)
+        first = aligned((chan * tiles + k) * inner, 8)
+        flags = mask_ref[pl.ds(first, inner), :].astype(F32)
+        decoded = lax.dot_general(
+            ub_rows[here, :], dec_ref[...], (((1,), (1,)), ((), ())), preferred_element_type=F32
         )
-        for n, (grad, weight, moment, square, rate) in enumerate(sets):
-            results = adamw(grad, weight[...], moment[...], square[...], rate)
-            for m in range(4):
-                updates[4 * n + m][...] = results[m]
+        valid = jnp.concatenate([columns[n % BANDS] * flags[n : n + 1, 0:1] for n in range(inner)], axis=0)
+        out_rows[here, :] = (decoded * valid).astype(BF16)
+        out_copy(k).start()
+        ig_copy(k).wait()
+        grad_copy(k).start()
+        return carry
+
+    lax.fori_loop(0, tiles, out_tile, 0)
+    for copy in arrive[2:]:
+        copy.wait()
+    q = q_ref[...]
+    heads, book = q[0:8], q[8:16]
+    high = lax.broadcasted_iota(jnp.int32, (8, 128), 1) >= LAT
+    gap = jnp.sum(jnp.where(high, q[16:24], 0.0))
+    count = jnp.sum(jnp.where(high, 0.0, q[16:24]))
+    ratio = jnp.full((8, 128), gap, F32) / jnp.full((8, 128), count * LAT, F32)
+    loss_ref[0] = ratio[0, 0]
+    loss_ref[1] = 0.25 * ratio[0, 0]
+    blocks = jnp.concatenate([g_ref[..., 0:LAT], g_ref[..., LAT:]], axis=1)
+    grads = (
+        blocks[0:9],
+        blocks[9],
+        heads[:, 0:LAT],
+        jnp.concatenate([book[:, 0:LAT], book[:, LAT:]], axis=0),
+        heads[:, LAT:],
+    )
+    for n, rate in enumerate((0.01, 0.03, 0.03, 0.5, 0.06)):
+        weight, moment, square = (ref[...] for ref in held[4 + 3 * n : 7 + 3 * n])
+        *values, low = adamw(grads[n], weight, moment, square, rate)
+        updates[4 * n + 3][...] = low
+        for m, value in enumerate(values):
+            results[3 * n + m][...] = value
+            leave[3 * n + m].start()
+    for copy in leave:
+        copy.wait()
+    for k in range(tiles):
+        grad_copy(k).wait()
+        out_copy(k).wait()
 
 
 def vmem():
@@ -672,13 +787,16 @@
         out_shape=(
             jax.ShapeDtypeStruct((pixels, 128), BF16),
             jax.ShapeDtypeStruct((pixels, channels), BF16),
-            jax.ShapeDtypeStruct((10, 32, LAT), F32),
+            jax.ShapeDtypeStruct((10, 16, 128), F32),
             jax.ShapeDtypeStruct((24, 128), F32),
             jax.ShapeDtypeStruct((channels, 128), BF16),
         ),
-        in_specs=[anywhere()] * 2 + [vmem()] * 7,
+        in_specs=[anywhere()] * 9,
         out_specs=(anywhere(), anywhere(), vmem(), vmem(), vmem()),
         scratch_shapes=[
+            pltpu.VMEM(ids.shape, jnp.int32),
+            pltpu.VMEM(mask.shape, jnp.int32),
+            *[pltpu.VMEM(block.shape, F32) for block in (conv_weight, point_weight, proj_weight, code_book, dec_weight)],
             pltpu.VMEM((pixels, channels), BF16),
             pltpu.VMEM((2, PITCH, channels), BF16),
             pltpu.VMEM((pixels, channels), BF16),
@@ -688,10 +806,10 @@
             pltpu.VMEM((pixels, 128), BF16),
             pltpu.VMEM((padded, channels), BF16),
             pltpu.VMEM((channels, pixels), BF16),
-            pltpu.VMEM((2, 10, 16, 128), BF16),
-            pltpu.VMEM((10, 16, 128), BF16),
             pltpu.VMEM((3, 2, 2, 2, 4, 3, 16, 128), BF16),
-            pltpu.VMEM((2, 2, 2, 4, 2, 16, 128), BF16),
+            pltpu.VMEM((2, 2, 2, 4, 16, 128), BF16),
+            pltpu.VMEM((2, 2, 2, 4, 16, 128), BF16),
+            pltpu.VMEM((pixels // 2, channels), F32),
             pltpu.VMEM((3, 3 * channels, channels), BF16),
             pltpu.VMEM((3, channels, 3 * channels), BF16),
             pltpu.VMEM((channels, channels), BF16),
@@ -707,26 +825,29 @@
             pltpu.VMEM((channels, channels), F32),
             pltpu.VMEM((entries, 128), F32),
             pltpu.VMEM((8, 128), F32),
-            pltpu.VMEM((2, 2, 2, 4, 40, 128), F32),
+            pltpu.VMEM((2, 2, 2, 4, 32, 128), F32),
+            pltpu.VMEM((2, 2, 2, 4, 8, 128), F32),
             pltpu.VMEM((3, 2, 2, 2, 4, 48, 128), F32),
-            pltpu.VMEM((2, 2, 4, 40, 128), F32),
-            pltpu.VMEM((3, 4, 40, 128), F32),
-            pltpu.VMEM((3, 40, 128), F32),
+            pltpu.VMEM((2, 2, 4, 32, 128), F32),
+            pltpu.VMEM((3, 4, 32, 128), F32),
+            pltpu.VMEM((3, 32, 128), F32),
+            pltpu.VMEM((2, 2, 4, 8, 128), F32),
+            pltpu.VMEM((3, 4, 8, 128), F32),
+            pltpu.VMEM((3, 8, 128), F32),
             pltpu.VMEM((3, 2, 2, 4, 48, 128), F32),
             pltpu.VMEM((3, 3, 4, 48, 128), F32),
             pltpu.VMEM((3, 3, 48, 128), F32),
-            pltpu.VMEM((10, 16, 128), F32),
-            pltpu.VMEM((10, 16, 128), F32),
+            dma((7,)),
             dma((chunks,)),
             dma((chunks,)),
-            dma((chunks,)),
+            dma((rows // BACK_ROWS,)),
             dma(()),
             dma((4,)),
             dma((4,)),
-            dma((4, 8)),
-            dma((4, 8)),
-            dma((4, 8)),
-            dma((4, 8)),
+            dma((5, 8)),
+            dma((5, 8)),
+            dma((5, 8)),
+            dma((5, 8)),
         ],
         compiler_params=pltpu.CompilerParams(
             collective_id=0, has_side_effects=True, vmem_limit_bytes=62 * 2**20
@@ -742,39 +863,39 @@
         proj_weight, proj_first, proj_second, code_book, code_first, code_second,
         dec_weight, dec_first, dec_second,
     )
-    tiles = pl.BlockSpec((CHUNK, channels), lambda n: (n, 0))
-
-    def whole(shape):
-        return pl.BlockSpec(shape, lambda n: (0,) * len(shape))
-
-    updates, specs = [], []
+    updates = []
     for n in range(5):
         shape = states[3 * n].shape
-        for kind in (F32, F32, F32, BF16):
-            updates.append(jax.ShapeDtypeStruct(shape, kind))
-            specs.append(whole(shape))
+        updates += [jax.ShapeDtypeStruct(shape, kind) for kind in (F32, F32, F32, BF16)]
+    smalls = (mask, decoder, grads, quant, *states)
+    tile = CHUNK
+    tiles = pixels // tile
     results = pl.pallas_call(
-        finish_kernel,
-        grid=(chunks,),
+        functools.partial(finish_kernel, tile),
         out_shape=(
             jax.ShapeDtypeStruct(inputs.shape, BF16),
             jax.ShapeDtypeStruct(inputs.shape, BF16),
             jax.ShapeDtypeStruct((2,), F32),
             *updates,
         ),
-        in_specs=[
-            tiles,
-            pl.BlockSpec((CHUNK, 128), lambda n: (n, 0)),
-            whole(mask.shape),
-            whole(decoder.shape),
-            whole(grads.shape),
-            whole(quant.shape),
-            *[whole(s.shape) for s in states],
+        in_specs=[anywhere()] * (2 + len(smalls)),
+        out_specs=(anywhere(), anywhere(), pl.BlockSpec(memory_space=pltpu.SMEM), *[anywhere() if n % 4 < 3 else vmem() for n in range(20)]),
+        scratch_shapes=[
+            pltpu.VMEM((pixels, 128), BF16),
+            pltpu.VMEM((pixels, channels), BF16),
+            pltpu.VMEM((pixels, channels), BF16),
+            *[pltpu.VMEM(block.shape, block.dtype) for block in smalls],
+            *[pltpu.VMEM(block.shape, F32) for n, block in enumerate(updates) if n % 4 < 3],
+            dma((tiles,)),
+            dma((tiles,)),
+            dma((tiles,)),
+            dma((tiles,)),
+            dma((len(smalls),)),
+            dma((15,)),
         ],
-        out_specs=(tiles, tiles, pl.BlockSpec(memory_space=pltpu.SMEM), *specs),
-        compiler_params=pltpu.CompilerParams(vmem_limit_bytes=62 * 2**20),
+        compiler_params=pltpu.CompilerParams(vmem_limit_bytes=61 * 2**20),
         name="finish",
-    )(ig, ub, mask, decoder, grads, quant, *states)
+    )(ig, ub, *smalls)
     point_new = tuple(block.T for block in results[7:11])
     return (*results[:7], *point_new, *results[11:])
 

time: 84.4 us -> 80.1 us (0.949)
  Pallas kernels: 83.3 us -> 79.2 us
    pallas_call x1, Pallas kernels: 75 us -> 72.6 us  [on_device(): pl.pallas_call(functools.partial(block_kernel, rows), out_shape=(jax.Shap...]
    pallas_call x1, Pallas kernels: 8.27 us -> 6.55 us  [on_device(): pl.pallas_call(functools.partial(finish_kernel, tile), out_shape=(jax.Sha...]
where the time goes in v3:
time: 80.1 us; the launch traced here: 80 us
  Pallas kernels  79.2 us (99%)
  between operations  0.83 us (1%)
    pallas_call x1, Pallas kernels, on_device(): pl.pallas_call(functools.partial(block_kernel, rows), out_shape=(jax.Shap...  72.6 us
    pallas_call x1, Pallas kernels, on_device(): pl.pallas_call(functools.partial(finish_kernel, tile), out_shape=(jax.Sha...  6.55 us

profile of v3, /device:TPU:0, one launch (start us, length us, event | category | flops | bytes accessed | tf_op | source)
XLA Modules:
  0.0 80.0 jit_solution(10527460502622017450)
XLA Ops:
  0.7 72.6 %block.1 = (bf16[8192,128]{1,0:T(8,128)(2,1)}, bf16[8192,256]{1,0:T(8,128)(2,1)}, f32[10,16,128]{2,1,0:T(8,128)}, f32[24,128]{1,0:T(8,128)}, bf16[256,128]{1,0:T(8,128)(2,1)}) custom-call(bf16[8192,256]{1,0:T(8,128)(2,1)} %x_hbm.1, bf16[8192,256]{1,0:T(8,128)(2,1)} %cot_hbm.1, s32[4,1,2048]{2,1,0:T(1,128)} %bitcast.13, s32[256,128]{1,0:T(8,128)} %bitcast.9, ...), custom_call_target="tpu_custom_call" | custom-call | tf_op jit(solution)/shard_map/block/pallas_call | solution.py:785
  73.3 6.5 %finish.1 = (bf16[8192,256]{1,0:T(8,128)(2,1)}, bf16[8192,256]{1,0:T(8,128)(2,1)}, f32[2]{0:T(128)}, f32[9,32,64]{2,1,0:T(8,128)}, f32[9,32,64]{2,1,0:T(8,128)},...) custom-call(bf16[8192,256]{1,0:T(8,128)(2,1)} %get-tuple-element.51., ...), custom_call_target="tpu_custom_call" | custom-call | tf_op jit(solution)/shard_map/finish/pallas_call | solution.py:873

commit v4 on v3

--- a/solution.py
+++ b/solution.py
@@ -84,7 +84,6 @@
     wb,
     pb,
     qb,
-    hidden_rows,
     wfull,
     wback,
     point_t,
@@ -262,18 +261,22 @@
         return wb.at[p - 1]
 
     def gather_z(p):
-        block = gather_buffer(p).at[core, xc, yc, zc]
+        buffer = gather_buffer(p)
+        block = buffer.at[core, :, :, zc] if p == 3 else buffer.at[core, xc, yc, zc]
         return [remote(block, block, ag_s.at[p, k], ag_r.at[p, k], z_peer[k]) for k in (1, 2, 3)]
 
     def gather_xy(p):
-        block = gather_buffer(p).at[core, xc, yc]
+        buffer = gather_buffer(p)
+        block = buffer.at[core, xc, yc, zc] if p == 3 else buffer.at[core, xc, yc]
         return [remote(block, block, ag_s.at[p, 3 + k], ag_r.at[p, 3 + k], xy_peer[k]) for k in (1, 2, 3)]
 
     def gather_core(p):
         block = gather_buffer(p).at[core]
         return [remote(block, block, ag_s.at[p, 7], ag_r.at[p, 7], core_peer)]
 
-    for p in (0, 1, 2, 3, 4):
+    start(gather_z(0))
+    start(gather_xy(3))
+    for p in (1, 2, 4):
         start(gather_z(p))
     halo_start(x_halo)
 
@@ -317,6 +320,8 @@
     lax.fori_loop(2, 5, shift_rows, 0)
     landed(gather_z(0))
     start(gather_xy(0))
+    landed(gather_xy(3))
+    start(gather_z(3))
     lax.fori_loop(5, rows // 4, shift_rows, 0)
     landed(gather_z(1))
     start(gather_xy(1))
@@ -332,11 +337,12 @@
     halo_row(0, 0, chan * rows - 1, chan > 0)
     halo_row(1, (rows + 1) * PITCH, jnp.minimum(chan * rows + rows, 3 * rows), chan < 3)
 
-    for p in (2, 3, 4):
-        landed(gather_z(p))
-        start(gather_xy(p))
+    landed(gather_z(2))
+    start(gather_xy(2))
     landed(gather_xy(0))
     start(gather_core(0))
+    landed(gather_z(4))
+    start(gather_xy(4))
 
     point_acc[...] = jnp.zeros_like(point_acc)
     book_acc[...] = jnp.zeros_like(book_acc)
@@ -396,6 +402,11 @@
             landed(gather_xy(1))
             start(gather_core(1))
 
+        @pl.when(k == 3)
+        def _():
+            landed(gather_z(3))
+            start(gather_core(3))
+
         return carry
 
     lax.fori_loop(0, chunks, decoder_step, 0)
@@ -416,23 +427,8 @@
         window = shifted[pl.ds(aligned((k * CHUNK_ROWS + i) * PITCH, PITCH), CHUNK), :]
         return dot(window, wfull[i])
 
-    def hidden_chunk(k, carry):
-        hidden_rows[rows_of(k), :] = taps(k, 0)
-
-        @pl.when(k == 0)
-        def _():
-            landed(gather_xy(2))
-            start(gather_core(2))
-
-        @pl.when(k == 1)
-        def _():
-            landed(gather_xy(3))
-            start(gather_core(3))
-
-        return carry
-
     def middle_chunk(k, carry):
-        hidden = hidden_rows[rows_of(k), :] + (taps(k, 1) + taps(k, 2))
+        hidden = taps(k, 0) + (taps(k, 1) + taps(k, 2))
         cotv[rows_of(k), :] = jnp.maximum(hidden, 0.0).astype(BF16)
 
         @pl.when(k == 0)
@@ -440,11 +436,6 @@
             landed(gather_xy(4))
             start(gather_core(4))
 
-        return carry
-
-    def whole_chunk(k, carry):
-        hidden = taps(k, 0) + (taps(k, 1) + taps(k, 2))
-        cotv[rows_of(k), :] = jnp.maximum(hidden, 0.0).astype(BF16)
         return carry
 
     def latent_chunk(k, carry):
@@ -473,12 +464,11 @@
         book_acc[...] += dot(onehot_t(k), u_rows[rows_of(k), :].astype(BF16))
         return carry
 
-    unpack_taps(0)
-    lax.fori_loop(0, chunks // 2, hidden_chunk, 0)
-    unpack_taps(1)
-    unpack_taps(2)
-    lax.fori_loop(0, chunks // 2, middle_chunk, 0)
-    lax.fori_loop(chunks // 2, chunks, whole_chunk, 0)
+    landed(gather_xy(2))
+    start(gather_core(2))
+    for i in (0, 2, 1):
+        unpack_taps(i)
+    lax.fori_loop(0, chunks, middle_chunk, 0)
     landed(gather_core(4))
     for x, y, z in squares:
         first = z * 64 + y * 32
@@ -809,7 +799,6 @@
             pltpu.VMEM((3, 2, 2, 2, 4, 3, 16, 128), BF16),
             pltpu.VMEM((2, 2, 2, 4, 16, 128), BF16),
             pltpu.VMEM((2, 2, 2, 4, 16, 128), BF16),
-            pltpu.VMEM((pixels // 2, channels), F32),
             pltpu.VMEM((3, 3 * channels, channels), BF16),
             pltpu.VMEM((3, channels, 3 * channels), BF16),
             pltpu.VMEM((channels, channels), BF16),

time: 80.1 us -> 79.5 us (level)
  no operation moved by 1% of the time
where the time goes in v4:
time: 79.5 us; the launch traced here: 79.4 us
  Pallas kernels  78.5 us (99%)
  between operations  0.83 us (1%)
    pallas_call x1, Pallas kernels, on_device(): pl.pallas_call(functools.partial(block_kernel, rows), out_shape=(jax.Shap...  72 us
    pallas_call x1, Pallas kernels, on_device(): pl.pallas_call(functools.partial(finish_kernel, tile), out_shape=(jax.Sha...  6.55 us

profile of v4, /device:TPU:0, one launch (start us, length us, event | category | flops | bytes accessed | tf_op | source)
XLA Modules:
  0.0 79.4 jit_solution(4496110803003675040)
XLA Ops:
  0.7 72.0 %block.1 = (bf16[8192,128]{1,0:T(8,128)(2,1)}, bf16[8192,256]{1,0:T(8,128)(2,1)}, f32[10,16,128]{2,1,0:T(8,128)}, f32[24,128]{1,0:T(8,128)}, bf16[256,128]{1,0:T(8,128)(2,1)}) custom-call(bf16[8192,256]{1,0:T(8,128)(2,1)} %x_hbm.1, bf16[8192,256]{1,0:T(8,128)(2,1)} %cot_hbm.1, s32[4,1,2048]{2,1,0:T(1,128)} %bitcast.13, s32[256,128]{1,0:T(8,128)} %bitcast.9, ...), custom_call_target="tpu_custom_call" | custom-call | tf_op jit(solution)/shard_map/block/pallas_call | solution.py:775
  72.6 6.5 %finish.1 = (bf16[8192,256]{1,0:T(8,128)(2,1)}, bf16[8192,256]{1,0:T(8,128)(2,1)}, f32[2]{0:T(128)}, f32[9,32,64]{2,1,0:T(8,128)}, f32[9,32,64]{2,1,0:T(8,128)},...) custom-call(bf16[8192,256]{1,0:T(8,128)(2,1)} %get-tuple-element.51., ...), custom_call_target="tpu_custom_call" | custom-call | tf_op jit(solution)/shard_map/finish/pallas_call | solution.py:862

commit v5 on v4

--- a/solution.py
+++ b/solution.py
@@ -81,6 +81,7 @@
     lg_rows,
     hgp,
     hgt,
+    resid_rows,
     wb,
     pb,
     qb,
@@ -118,6 +119,8 @@
     ub_sem,
     halo_s,
     halo_r,
+    q_s,
+    q_r,
     ag_s,
     ag_r,
     rs_s,
@@ -153,8 +156,8 @@
             copy.wait_send()
 
     barrier = pltpu.get_barrier_semaphore()
-    partners = [core_peer, (dp, 3 - chan)]
-    partners += xy_peer[1:] + z_peer[1:]
+    chip_peer = [(2 * z_of[k // 4] + xy_of[k % 4][1], 2 * xy_of[k % 4][0] + core) for k in range(16)]
+    partners = [core_peer, (dp, 3 - chan)] + chip_peer[1:]
     for partner in partners:
         pl.semaphore_signal(barrier, inc=1, device_id=partner, device_id_type=MESH)
 
@@ -270,11 +273,15 @@
         block = buffer.at[core, xc, yc, zc] if p == 3 else buffer.at[core, xc, yc]
         return [remote(block, block, ag_s.at[p, 3 + k], ag_r.at[p, 3 + k], xy_peer[k]) for k in (1, 2, 3)]
 
+    def quant_copies():
+        block = qb.at[core, xc, yc, zc]
+        return [remote(block, block, q_s.at[k], q_r.at[k], chip_peer[k]) for k in range(1, 16)]
+
     def gather_core(p):
         block = gather_buffer(p).at[core]
         return [remote(block, block, ag_s.at[p, 7], ag_r.at[p, 7], core_peer)]
 
-    start(gather_z(0))
+    start(quant_copies())
     start(gather_xy(3))
     for p in (1, 2, 4):
         start(gather_z(p))
@@ -318,13 +325,13 @@
     for k in range(1, chunks):
         x_copy(k).wait()
     lax.fori_loop(2, 5, shift_rows, 0)
-    landed(gather_z(0))
-    start(gather_xy(0))
     landed(gather_xy(3))
     start(gather_z(3))
     lax.fori_loop(5, rows // 4, shift_rows, 0)
     landed(gather_z(1))
     start(gather_xy(1))
+    landed(quant_copies())
+    start(gather_core(0))
     halo_wait_recv(x_halo)
 
     def halo_row(side, at, global_row, present):
@@ -337,16 +344,11 @@
     halo_row(0, 0, chan * rows - 1, chan > 0)
     halo_row(1, (rows + 1) * PITCH, jnp.minimum(chan * rows + rows, 3 * rows), chan < 3)
 
+
+    book_acc[...] = jnp.zeros_like(book_acc)
+    loss_acc[...] = jnp.zeros_like(loss_acc)
     landed(gather_z(2))
     start(gather_xy(2))
-    landed(gather_xy(0))
-    start(gather_core(0))
-    landed(gather_z(4))
-    start(gather_xy(4))
-
-    point_acc[...] = jnp.zeros_like(point_acc)
-    book_acc[...] = jnp.zeros_like(book_acc)
-    loss_acc[...] = jnp.zeros_like(loss_acc)
     landed(gather_core(0))
 
     squares = [(x, y, z) for z in range(4) for y in range(2) for x in range(2)]
@@ -396,6 +398,11 @@
     def decoder_step(k, carry):
         cot_copy(k).wait()
         decoder_chunk(k)
+
+        @pl.when(k == 0)
+        def _():
+            landed(gather_z(4))
+            start(gather_xy(4))
 
         @pl.when(k == 2)
         def _():
@@ -453,7 +460,7 @@
         coarse = term.astype(BF16).astype(F32)
         u_rows[rows_of(k), :] = jnp.where(high, coarse, pltpu.roll(term - coarse, LAT, 1))
         resid_low = dot(latent_grad, proj_t[...]).astype(BF16)
-        point_acc[...] += dot_rows(resid_low, middle)
+        resid_rows[rows_of(k), :] = resid_low
         back = dot(resid_low, point_t[...])
         hidden_grad = jnp.where(middle.astype(F32) > 0.0, back, 0.0).astype(BF16)
         hgp[pl.ds(aligned((k * CHUNK_ROWS + 1) * PITCH, PITCH), CHUNK), :] = hidden_grad
@@ -594,6 +601,7 @@
         return carry
 
     proj_acc[...] = dot_rows(lg_rows[...], xv[...]).T
+    point_acc[...] = dot_rows(resid_rows[...], cotv[...])
     pack_small()
     start(reduce_core(0))
     lax.fori_loop(0, 3, grad_step, 0)
@@ -654,8 +662,10 @@
         out_copy(k).wait()
     halo_wait_send(x_halo)
     halo_wait_send(hg_halo)
+    sent(quant_copies() + gather_core(0))
+    for p in range(1, 5):
+        sent(gather_z(p) + gather_xy(p) + gather_core(p))
     for p in range(5):
-        sent(gather_z(p) + gather_xy(p) + gather_core(p))
         sent(reduce_core(p) + reduce_xy(p) + reduce_z(p))
 
 
@@ -796,6 +806,7 @@
             pltpu.VMEM((pixels, 128), BF16),
             pltpu.VMEM((padded, channels), BF16),
             pltpu.VMEM((channels, pixels), BF16),
+            pltpu.VMEM((pixels, channels), BF16),
             pltpu.VMEM((3, 2, 2, 2, 4, 3, 16, 128), BF16),
             pltpu.VMEM((2, 2, 2, 4, 16, 128), BF16),
             pltpu.VMEM((2, 2, 2, 4, 16, 128), BF16),
@@ -833,6 +844,8 @@
             dma(()),
             dma((4,)),
             dma((4,)),
+            dma((16,)),
+            dma((16,)),
             dma((5, 8)),
             dma((5, 8)),
             dma((5, 8)),

time: 79.5 us -> 78.7 us (0.990)
  Pallas kernels: 78.5 us -> 77.7 us
    pallas_call x1, Pallas kernels: 72 us -> 71.1 us  [on_device(): pl.pallas_call(functools.partial(block_kernel, rows), out_shape=(jax.Shap...]
where the time goes in v5:
time: 78.7 us; the launch traced here: 78.5 us
  Pallas kernels  77.7 us (99%)
  between operations  0.83 us (1%)
    pallas_call x1, Pallas kernels, on_device(): pl.pallas_call(functools.partial(block_kernel, rows), out_shape=(jax.Shap...  71.1 us
    pallas_call x1, Pallas kernels, on_device(): pl.pallas_call(functools.partial(finish_kernel, tile), out_shape=(jax.Sha...  6.55 us

profile of v5, /device:TPU:0, one launch (start us, length us, event | category | flops | bytes accessed | tf_op | source)
XLA Modules:
  0.0 78.5 jit_solution(11436702992437974850)
XLA Ops:
  0.7 71.1 %block.1 = (bf16[8192,128]{1,0:T(8,128)(2,1)}, bf16[8192,256]{1,0:T(8,128)(2,1)}, f32[10,16,128]{2,1,0:T(8,128)}, f32[24,128]{1,0:T(8,128)}, bf16[256,128]{1,0:T(8,128)(2,1)}) custom-call(bf16[8192,256]{1,0:T(8,128)(2,1)} %x_hbm.1, bf16[8192,256]{1,0:T(8,128)(2,1)} %cot_hbm.1, s32[4,1,2048]{2,1,0:T(1,128)} %bitcast.13, s32[256,128]{1,0:T(8,128)} %bitcast.9, ...), custom_call_target="tpu_custom_call" | custom-call | tf_op jit(solution)/shard_map/block/pallas_call | solution.py:785
  71.8 6.5 %finish.1 = (bf16[8192,256]{1,0:T(8,128)(2,1)}, bf16[8192,256]{1,0:T(8,128)(2,1)}, f32[2]{0:T(128)}, f32[9,32,64]{2,1,0:T(8,128)}, f32[9,32,64]{2,1,0:T(8,128)},...) custom-call(bf16[8192,256]{1,0:T(8,128)(2,1)} %get-tuple-element.51., ...), custom_call_target="tpu_custom_call" | custom-call | tf_op jit(solution)/shard_map/finish/pallas_call | solution.py:875
